TPU v7x, 512 devices: a whole 4x8x8 slice. The times are simulated.
512 devices in a mesh: passage: 32 (over x, y), sub: 16 (over z, core).
Axes of the slice: x: 4, y: 8, z: 8, core: 2. Of those that a mesh axis runs over, the one named last changes fastest.
Arguments:
- block_vectors: float32 [32, 131072], P(None, ('passage', 'sub')), may hold values from -75 to 75
- stiffness: float32 [131072], P(('passage', 'sub')), may hold values from 2 to 8
- mass_diag: float32 [131072], P(('passage', 'sub')), may hold values from 0.5 to 2
- kblocks: float32 [1024, 4, 128, 128], P(('passage', 'sub')), may hold values from -0.25 to 0.25
- block_cols: int32 [1024, 4], P(('passage', 'sub')), may hold values from 0 to 5
- slot_node: int32 [524288], P(('passage', 'sub')), may hold values from 0 to 255
- slot_owner: int32 [524288, 1], P(('passage', 'sub')), may hold values from 0 to 15; in each aligned block of 1024 rows (0 to 1023, 1024 to 2047, ...) at most 128 rows name the same one
- slot_cell: int32 [524288], P(('passage', 'sub')), may hold values from 0 to 8191
- slot_weight: float32 [524288], P(('passage', 'sub')), may hold values from 0.5 to 4
- live_slots: int32 [512], P(('passage', 'sub')), may hold values from 768 to 1024, as said below
Outputs:
- residual: float32 [32, 131072], P(None, ('passage', 'sub'))
- gram_stiff: float32 [64, 64], replicated
- gram_plain: float32 [64, 64], replicated
Inputs may be any that keep to these rules, and one draw needn't show every extreme that they name: `slot_owner`: per device at most 128 slots name the same owner, and some device reaches 128 for some owner. `live_slots`: some device has all 1024 slots live.
All inputs are finite; a program needn't handle non-finite values.
Results may differ from a plain program's by a relative error of at most 0.00019.
Values sent between devices are 32-bit elements; how exact they have to be, the bound alone decides.
A program may use at most 64 MiB of HBM per device.

v0:
```python
import jax
import jax.numpy as jnp
from jax import lax
from jax.sharding import PartitionSpec as P

CX = 8
CY = 8
CZ = 128


center_weight = 15.0
lower_bound = 1.0 / 15.0
upper_bound = 17.0 / 15.0
middle = (upper_bound + lower_bound) / 2.0
radius = (upper_bound - lower_bound) / 2.0
sigma_ratio = middle / radius
first_rho = 1.0 / sigma_ratio
second_rho = 1.0 / (2.0 * sigma_ratio - first_rho)
third_rho = 1.0 / (2.0 * sigma_ratio - second_rho)


def padded_2(block, sides, width, periodic):
    for axis, dim in sides:
        count = lax.axis_size(axis)
        forward = [(i, i + 1) for i in range(count - 1)]
        if periodic:
            forward.append((count - 1, 0))
        backward = [(target, source) for source, target in forward]
        low = lax.ppermute(
            lax.slice_in_dim(block, block.shape[dim] - width, None, axis=dim), axis, forward
        )
        high = lax.ppermute(lax.slice_in_dim(block, 0, width, axis=dim), axis, backward)
        block = jnp.concatenate([low, block, high], axis=dim)
    return block


def laplace_inner(padded):
    rows_one = padded.shape[1] - 2
    rows_two = padded.shape[2] - 2
    depth = padded.shape[3]
    zpadded = jnp.pad(padded, ((0, 0), (0, 0), (0, 0), (1, 1)))
    neighbours = jnp.zeros((padded.shape[0], rows_one, rows_two, depth), jnp.float32)
    for offset_one in range(3):
        for offset_two in range(3):
            for offset_three in range(3):
                distance = abs(offset_one - 1) + abs(offset_two - 1) + abs(offset_three - 1)
                if distance == 0:
                    continue
                weight = 0.5 ** (distance - 1)
                neighbours = (
                    neighbours
                    + weight
                    * zpadded[
                        :,
                        offset_one : offset_one + rows_one,
                        offset_two : offset_two + rows_two,
                        offset_three : offset_three + depth,
                    ]
                )
    return center_weight * padded[:, 1:-1, 1:-1, :] - neighbours


def extend_field(field):
    wider = padded_2(field, (("passage", 1),), 1, True)
    return padded_2(wider, (("sub", 2),), 1, False)


def pressure_solve(source):
    first = source / (center_weight * middle)
    resid = source - laplace_inner(extend_field(first))
    second_step = second_rho * first_rho * first + 2.0 * second_rho / radius * (
        resid / center_weight
    )
    second = first + second_step
    resid = source - laplace_inner(extend_field(second))
    third_step = third_rho * second_rho * second_step + 2.0 * third_rho / radius * (
        resid / center_weight
    )
    result = second + third_step
    return result


def stiffness_apply(field, block_cols, kblocks, stiffness):
    width, local = field.shape
    block_size = kblocks.shape[2]
    window = padded_2(field, (("sub", 1),), local, False)
    blocks = window.reshape(width, 3 * local // block_size, block_size)
    gathered = blocks[:, block_cols]
    mixed = jnp.einsum("mrnb,rnbk->mrk", gathered, kblocks, precision=lax.Precision.HIGHEST)
    return stiffness[None, :] * field + mixed.reshape(width, local)


def inner(left, right):
    return lax.dot_general(
        left,
        right,
        (((1,), (1,)), ((), ())),
        precision=lax.Precision.HIGHEST,
        preferred_element_type=jnp.float32,
    )


def body(
    block_vectors,
    stiffness,
    mass_diag,
    kblocks,
    block_cols,
    slot_node,
    slot_owner,
    slot_cell,
    slot_weight,
    live_slots,
):
    modes, local = block_vectors.shape
    groups = lax.axis_size("sub")
    slots = slot_node.shape[0]
    capacity = 2 * slots // groups
    total = local * lax.axis_size("passage") * groups
    live = (jnp.arange(slots, dtype=jnp.int32) < live_slots[0]).astype(jnp.float32)
    scaled = slot_weight * live
    owner = slot_owner[:, 0]
    onehot = (owner[:, None] == jnp.arange(groups, dtype=jnp.int32)[None, :]).astype(jnp.int32)
    before = jnp.cumsum(onehot, axis=0) - onehot
    target = owner * capacity + jnp.sum(before * onehot, axis=1)
    cells_out = (
        jnp.zeros((groups * capacity,), jnp.int32)
        .at[target]
        .set(slot_cell)
        .reshape(groups, capacity)
    )
    cells_in = lax.all_to_all(cells_out, "sub", split_axis=0, concat_axis=0, tiled=True).reshape(-1)
    stiff_image = stiffness_apply(block_vectors, block_cols, kblocks, stiffness)
    values = block_vectors[:, slot_node] * scaled[None, :]
    outgoing = (
        jnp.zeros((modes, groups * capacity), jnp.float32)
        .at[:, target]
        .set(values)
        .reshape(modes, groups, capacity)
    )
    incoming = lax.all_to_all(outgoing, "sub", split_axis=1, concat_axis=1, tiled=True).reshape(
        modes, -1
    )
    source = (
        jnp.zeros((modes, CX * CY * CZ), jnp.float32)
        .at[:, cells_in]
        .add(incoming)
        .reshape(modes, CX, CY, CZ)
    )
    press = pressure_solve(source).reshape(modes, -1)
    picked = press[:, cells_in].reshape(modes, groups, capacity)
    returned = lax.all_to_all(picked, "sub", split_axis=1, concat_axis=1, tiled=True).reshape(
        modes, -1
    )
    forces = returned[:, target] * scaled[None, :]
    mass_image = mass_diag[None, :] * block_vectors + jnp.zeros((modes, local), jnp.float32).at[
        :, slot_node
    ].add(forces)
    numer, denom = lax.psum(
        (jnp.sum(block_vectors * stiff_image, axis=1), jnp.sum(block_vectors * mass_image, axis=1)),
        ("passage", "sub"),
    )
    theta = numer / denom
    residual = stiff_image - theta[:, None] * mass_image
    stiff_resid = stiffness_apply(residual, block_cols, kblocks, stiffness)
    search = jnp.concatenate([block_vectors, residual], axis=0)
    image = jnp.concatenate([stiff_image, stiff_resid], axis=0)
    gram_stiff, gram_plain = lax.psum(
        (inner(search, image), inner(search, search)), ("passage", "sub")
    )
    return (residual, gram_stiff / total, gram_plain / total)


def solution(mesh):
    return jax.shard_map(
        body,
        mesh=mesh,
        in_specs=(
            P(None, ("passage", "sub")),
            P(("passage", "sub")),
            P(("passage", "sub")),
            P(("passage", "sub"), None, None, None),
            P(("passage", "sub"), None),
            P(("passage", "sub")),
            P(("passage", "sub"), None),
            P(("passage", "sub")),
            P(("passage", "sub")),
            P(("passage", "sub")),
        ),
        out_specs=(P(None, ("passage", "sub")), P(), P()),
        check_vma=False,
    )
```

profile of v0, /device:TPU:1, one launch (start us, length us, event | category | flops | bytes accessed | tf_op | source)
XLA Modules:
  0.0 408.0 jit_solution(4970201615528179702)
XLA Ops:
  1.4 4.5 %reduce-window.6 = s32[16,8,128]{2,1,0:T(8,128)S(1)} reduce-window(s32[16,8,128]{2,1,0:T(8,128)S(1)} %fusion.68, s32[]{:T(128)} %constant.17.clone.1), window={size=1x1x128 pad=0_0x0_0x127_0}, to_apply=%region_2.3 | reduce-window | flops 2080768 | bytes 131076 | tf_op jit(solution)/shard_map/reduce-window
  7.7 5.0 %scatter_custom_fusion = s32[2048]{0:T(1024)} fusion(s32[1024]{0:T(1024)S(1)} %bitcast.91, s32[1024]{0:T(1024)} %param.17, s32[]{:T(128)} %constant.17.clone.1), kind=kCustom, calls=%fused_computation.178 | custom fusion | bytes 8704 | tf_op jit(solution)/shard_map/scatter | solution.py:129
  12.8 11.8 %all-to-all-start = ((s32[16,1,128]{2,1,0:T(1,128)}), s32[16,1,128]{2,1,0:T(1,128)S(1)}, u32[]{:S(2)}, u32[]{:S(2)}) async-start(s32[16,1,128]{2,1,0:T(1,128)} %bitcast.12), calls=%async_computation | async-start | bytes 16384 | tf_op jit(solution)/shard_map/all_to_all | solution.py:132
  28.1 6.6 %scatter_custom_fusion.1 = f32[32,2048]{0,1:T(8,128)S(1)} fusion(s32[1024]{0:T(1024)S(1)} %bitcast.92, f32[]{:T(128)} %constant.19.clone.1, f32[1024]{0:T(1024)S(1)} %fusion.72, f32[32,256]{0,1:T(8,128)S(1)} %copy.184, s32[1024]{0:T(1024)S(1)} %get-tuple-element.42), kind=kCustom, calls=%fused_computation.133 | custom fusion | flops 32768 | bytes 401412 | tf_op jit(solution)/shard_map/scatter | solution.py:138
  35.7 7.2 %all-to-all-start.1 = ((f32[32,16,128]{2,0,1:T(8,128)}), f32[32,16,128]{2,0,1:T(8,128)S(1)}, u32[]{:S(2)}, u32[]{:S(2)}) async-start(f32[32,16,128]{2,0,1:T(8,128)} %copy.192), calls=%async_computation.1 | async-start | bytes 524288 | tf_op jit(solution)/shard_map/all_to_all | solution.py:141
  42.9 11.7 %all-to-all-done.1 = f32[32,16,128]{2,0,1:T(8,128)S(1)} async-done(((f32[32,16,128]{2,0,1:T(8,128)}), f32[32,16,128]{2,0,1:T(8,128)S(1)}, u32[]{:S(2)}, u32[]{:S(2)}) %all-to-all-start.1) | async-done | bytes 262176 | tf_op jit(solution)/shard_map/all_to_all | solution.py:141
  55.0 15.5 %scatter_custom_fusion.2 = f32[32,8192]{0,1:T(8,128)} fusion(s32[2048]{0:T(1024)S(1)} %bitcast.87, f32[2048,32]{1,0:T(8,128)S(1)} %copy.194, f32[]{:T(128)} %constant.19.clone.1), kind=kCustom, calls=%fused_computation.24 | custom fusion | flops 65536 | bytes 1048580 | tf_op jit(solution)/shard_map/scatter-add | solution.py:147
  70.5 3.1 copy.195
  76.7 6.3 %collective-permute-start.3 = (f32[32,1,8,128]{3,2,1,0:T(8,128)S(1)}, f32[32,1,8,128]{3,2,1,0:T(8,128)S(1)}, u32[]{:S(2)}, u32[]{:S(2)}) collective-permute-start(f32[32,1,8,128]{3,2,1,0:T(8,128)S(1)} %get-tuple-element.41), channel_id=1, source_target_pairs={{16,0},{32,16},{48,32},{64,48},{80,64},{96,80},{112,96},{128,112},... | collective-permute-start | bytes 393224 | tf_op jit(solution)/shard_map/ppermute | solution.py:32
  101.6 5.4 %select_maximum_fusion.4 = f32[32,10,10,130]{3,2,1,0:T(8,128)} fusion(f32[32,10,1,128]{3,2,1,0:T(1,128)S(1)} %copy.201, f32[32,10,1,128]{3,2,1,0:T(1,128)S(1)} %copy.200, f32[32,1,8,128]{3,2,1,0:T(8,128)S(1)} %collective-permute-done.3, f32[32,8,8,128]{3,2,1,0:T(8,128)S(1)} %broadcast_multiply_fusion, f32[32,1,8,128]{3,2,1,0:T(8,128)S(1)} %collective-permute-done.2), kind=kLoop, calls=%fused_computation.15 | loop fusion | flops 4992000 | bytes 3302400 | tf_op jit(solution)/shard_map/concatenate | solution.py:33
  106.9 23.2 %fusion.77 = (f32[32,8,8,128]{3,2,1,0:T(8,128)S(1)}, f32[32,8,8,128]{3,2,1,0:T(8,128)}) fusion(f32[32,8,8,128]{3,2,1,0:T(8,128)} %copy-done.1, f32[32,10,10,130]{3,2,1,0:T(8,128)} %select_maximum_fusion.4, f32[32,10,9,128]{3,2,1,0:T(8,128)} %get-tuple-element.35, f32[32,1,8,128]{3,2,1,0:T(8,128)S(1)} %collective-permute-done.3, ...), kind=kLoop, calls=%fused_computation.188 | loop fusion | flops 14417920 | bytes 29622272 | tf_op jit(solution)/shard_map/add | solution.py:74
  132.1 6.7 %collective-permute-start.7 = (f32[32,1,8,128]{3,2,1,0:T(8,128)S(1)}, f32[32,1,8,128]{3,2,1,0:T(8,128)S(1)}, u32[]{:S(2)}, u32[]{:S(2)}) collective-permute-start(f32[32,1,8,128]{3,2,1,0:T(8,128)S(1)} %get-tuple-element.39), channel_id=1, source_target_pairs={{16,0},{32,16},{48,32},{64,48},{80,64},{96,80},{112,96},{128,112},... | collective-permute-start | bytes 393224 | tf_op jit(solution)/shard_map/ppermute | solution.py:32
  146.2 4.2 %collective-permute-done.9 = f32[32,10,1,128]{3,0,2,1:T(8,128)S(1)} collective-permute-done((f32[32,10,1,128]{3,0,2,1:T(8,128)S(1)}, f32[32,10,1,128]{3,0,2,1:T(8,128)S(1)}, u32[]{:S(2)}, u32[]{:S(2)}) %collective-permute-start.9) | collective-permute-done | bytes 163872 | tf_op jit(solution)/shard_map/ppermute | solution.py:32
  152.8 3.9 select_maximum_fusion
  156.7 6.5 %fusion.8 = f32[32,8,8,128]{3,2,1,0:T(8,128)} fusion(f32[32,8,8,128]{3,2,1,0:T(8,128)S(1)} %get-tuple-element.28, f32[32,8,8,128]{3,2,1,0:T(8,128)S(1)} %copy-done.2, f32[32,10,10,130]{3,2,1,0:T(8,128)S(1)} %select_maximum_fusion, f32[32,10,9,128]{3,2,1,0:T(8,128)} %get-tuple-element.31, f32[32,1,8,128]{3,2,1,0:T(8,128)S(1)} %collective-permute-done.7, ...), kind=kLoop, calls=%fused_computation.34 | loop fusion | flops 14155776 | bytes 29622272 | tf_op jit(solution)/shard_map/add | solution.py:79
  163.2 3.6 copy.212
  166.9 7.7 %gather_fusion.1 = f32[2048,32]{1,0:T(8,128)S(1)} fusion(f32[32,8192]{0,1:T(8,128)} %bitcast.78, s32[2048]{0:T(1024)S(1)} %broadcast_clamp_fusion), kind=kCustom, calls=%fused_computation.2 | custom fusion | bytes 532480 | tf_op jit(solution)/shard_map/gather | solution.py:151
  175.6 6.7 %all-to-all-start.2 = ((f32[32,16,128]{2,0,1:T(8,128)}), f32[32,16,128]{2,0,1:T(8,128)S(1)}, u32[]{:S(2)}, u32[]{:S(2)}) async-start(f32[32,16,128]{2,0,1:T(8,128)} %copy.213), calls=%async_computation.2 | async-start | bytes 524288 | tf_op jit(solution)/shard_map/all_to_all | solution.py:152
  184.3 9.7 %all-to-all-done.2 = f32[32,16,128]{2,0,1:T(8,128)S(1)} async-done(((f32[32,16,128]{2,0,1:T(8,128)}), f32[32,16,128]{2,0,1:T(8,128)S(1)}, u32[]{:S(2)}, u32[]{:S(2)}) %all-to-all-start.2) | async-done | bytes 262176 | tf_op jit(solution)/shard_map/all_to_all | solution.py:152
  194.3 9.7 %scatter_custom_fusion.3 = f32[32,256]{0,1:T(8,128)S(1)} fusion(f32[32,256]{0,1:T(8,128)S(1)} %copy.215, s32[1024]{0:T(1024)} %get-tuple-element.43, f32[1024]{0:T(1024)S(1)} %fusion.72, f32[32,2048]{0,1:T(8,128)S(1)} %bitcast.79, s32[1024]{0:T(1024)S(1)} %broadcast_clamp_fusion.1), kind=kCustom, calls=%fused_computation.131 | custom fusion | flops 65536 | bytes 1089536 | tf_op jit(solution)/shard_map/scatter-add | solution.py:158
  204.1 96.8 %all-reduce.3 = (f32[32]{0:T(128)S(1)}, f32[32]{0:T(128)S(1)}) all-reduce(f32[32]{0:T(128)S(1)} %get-tuple-element.22, f32[32]{0:T(128)S(1)} %get-tuple-element.21), channel_id=1, replica_groups=mesh['passage'=32,'sub'=16] {'passage','sub'}, use_global_device_ids=true, to_apply=%region_1.2 | all-reduce | flops 64 | bytes 512 | tf_op jit(solution)/shard_map/psum | solution.py:159
  301.0 3.8 collective-permute-start.10
  307.4 3.7 collective-permute-done.11
  312.8 94.6 %all-reduce.2 = (f32[64,64]{1,0:T(8,128)S(1)}, f32[64,64]{1,0:T(8,128)S(1)}) all-reduce(f32[64,64]{1,0:T(8,128)S(1)} %fusion.61, f32[64,64]{1,0:T(8,128)S(1)} %fusion.69), channel_id=1, replica_groups=mesh['passage'=32,'sub'=16] {'passage','sub'}, use_global_device_ids=true, to_apply=%region_11.12 | all-reduce | flops 8192 | bytes 65536 | tf_op jit(solution)/shard_map/psum | solution.py:168
  (98 shorter events, 48.5 us)
Async XLA Ops:
  0.6 183.1 %copy-start = (f32[2,4,128,128]{3,2,1,0:T(8,128)S(1)}, f32[2,4,128,128]{3,2,1,0:T(8,128)}, u32[]{:S(2)}) copy-start(f32[2,4,128,128]{3,2,1,0:T(8,128)} %param.13) | copy-start | bytes 1572868
  12.8 22.9 %all-to-all-start = ((s32[16,1,128]{2,1,0:T(1,128)}), s32[16,1,128]{2,1,0:T(1,128)S(1)}, u32[]{:S(2)}, u32[]{:S(2)}) async-start(s32[16,1,128]{2,1,0:T(1,128)} %bitcast.12), calls=%async_computation | async-start | bytes 16384 | tf_op jit(solution)/shard_map/all_to_all | solution.py:132
  35.7 18.9 %all-to-all-start.1 = ((f32[32,16,128]{2,0,1:T(8,128)}), f32[32,16,128]{2,0,1:T(8,128)S(1)}, u32[]{:S(2)}, u32[]{:S(2)}) async-start(f32[32,16,128]{2,0,1:T(8,128)} %copy.192), calls=%async_computation.1 | async-start | bytes 524288 | tf_op jit(solution)/shard_map/all_to_all | solution.py:141
  70.5 12.4 %copy-start.4 = (f32[32,256]{1,0:T(8,128)S(1)}, f32[32,256]{1,0:T(8,128)}, u32[]{:S(2)}) copy-start(f32[32,256]{1,0:T(8,128)} %param.10) | copy-start | bytes 98308
  73.6 28.0 %copy-start.1 = (f32[32,8,8,128]{3,2,1,0:T(8,128)}, f32[32,8,8,128]{3,2,1,0:T(8,128)S(1)}, u32[]{:S(2)}) copy-start(f32[32,8,8,128]{3,2,1,0:T(8,128)S(1)} %copy.195) | copy-start | bytes 3145732
  73.6 19.3 %copy-start.8 = (s32[2,4]{1,0:T(2,128)S(1)}, s32[2,4]{1,0:T(2,128)}, u32[]{:S(2)}) copy-start(s32[2,4]{1,0:T(2,128)} %param.14) | copy-start | bytes 100
  73.8 14.1 %collective-permute-start.2 = (f32[32,1,8,128]{3,2,1,0:T(8,128)S(1)}, f32[32,1,8,128]{3,2,1,0:T(8,128)S(1)}, u32[]{:S(2)}, u32[]{:S(2)}) collective-permute-start(f32[32,1,8,128]{3,2,1,0:T(8,128)S(1)} %get-tuple-element.40), channel_id=1, source_target_pairs={{0,16},{16,32},{32,48},{48,64},{64,80},{80,96},{96,112},{112,128},... | collective-permute-start | bytes 393224 | tf_op jit(solution)/shard_map/ppermute | solution.py:29
  76.7 11.2 %collective-permute-start.3 = (f32[32,1,8,128]{3,2,1,0:T(8,128)S(1)}, f32[32,1,8,128]{3,2,1,0:T(8,128)S(1)}, u32[]{:S(2)}, u32[]{:S(2)}) collective-permute-start(f32[32,1,8,128]{3,2,1,0:T(8,128)S(1)} %get-tuple-element.41), channel_id=1, source_target_pairs={{16,0},{32,16},{48,32},{64,48},{80,64},{96,80},{112,96},{128,112},... | collective-permute-start | bytes 393224 | tf_op jit(solution)/shard_map/ppermute | solution.py:32
  82.9 99.4 %collective-permute-start = (f32[32,256]{1,0:T(8,128)S(1)}, f32[32,256]{1,0:T(8,128)}, u32[]{:S(2)}, u32[]{:S(2)}) collective-permute-start(f32[32,256]{1,0:T(8,128)S(1)} %copy-done.4), channel_id=1, source_target_pairs={{0,1},{1,2},{2,3},{3,4},{4,5},{5,6},{6,7},{7,8},{8,9},{9,10},{10,1... | collective-permute-start | bytes 98312 | tf_op jit(solution)/shard_map/ppermute | solution.py:29
  84.9 97.5 %collective-permute-start.1 = (f32[32,256]{1,0:T(8,128)S(1)}, f32[32,256]{1,0:T(8,128)}, u32[]{:S(2)}, u32[]{:S(2)}) collective-permute-start(f32[32,256]{1,0:T(8,128)S(1)} %copy-done.4), channel_id=1, source_target_pairs={{1,0},{2,1},{3,2},{4,3},{5,4},{6,5},{7,6},{8,7},{9,8},{10,9},{11,1... | collective-permute-start | bytes 98312 | tf_op jit(solution)/shard_map/ppermute | solution.py:32
  88.1 6.6 %collective-permute-start.4 = (f32[32,10,1,128]{3,0,2,1:T(8,128)S(1)}, f32[32,10,1,128]{3,0,2,1:T(8,128)S(1)}, u32[]{:S(2)}, u32[]{:S(2)}) collective-permute-start(f32[32,10,1,128]{3,0,2,1:T(8,128)S(1)} %copy.231), channel_id=1, source_target_pairs={{0,1},{1,2},{2,3},{3,4},{4,5},{5,6},{6,7},{7,8},{8,9},{9,10},{10,1... | collective-permute-start | bytes 491528 | tf_op jit(solution)/shard_map/ppermute | solution.py:29
  90.7 6.7 %collective-permute-start.5 = (f32[32,10,1,128]{3,0,2,1:T(8,128)S(1)}, f32[32,10,1,128]{3,0,2,1:T(8,128)}, u32[]{:S(2)}, u32[]{:S(2)}) collective-permute-start(f32[32,10,1,128]{3,0,2,1:T(8,128)S(1)} %copy.232), channel_id=1, source_target_pairs={{1,0},{2,1},{3,2},{4,3},{5,4},{6,5},{7,6},{8,7},{9,8},{10,9},{11,1... | collective-permute-start | bytes 491528 | tf_op jit(solution)/shard_map/ppermute | solution.py:32
  106.9 31.8 %copy-start.7 = (f32[256]{0:T(256)S(1)}, f32[256]{0:T(256)}, u32[]{:S(2)}) copy-start(f32[256]{0:T(256)} %param.12) | copy-start | bytes 3076
  130.1 9.0 %collective-permute-start.6 = (f32[32,1,8,128]{3,2,1,0:T(8,128)S(1)}, f32[32,1,8,128]{3,2,1,0:T(8,128)S(1)}, u32[]{:S(2)}, u32[]{:S(2)}) collective-permute-start(f32[32,1,8,128]{3,2,1,0:T(8,128)S(1)} %get-tuple-element.38), channel_id=1, source_target_pairs={{0,16},{16,32},{32,48},{48,64},{64,80},{80,96},{96,112},{112,128},... | collective-permute-start | bytes 393224 | tf_op jit(solution)/shard_map/ppermute | solution.py:29
  132.1 8.6 %collective-permute-start.7 = (f32[32,1,8,128]{3,2,1,0:T(8,128)S(1)}, f32[32,1,8,128]{3,2,1,0:T(8,128)S(1)}, u32[]{:S(2)}, u32[]{:S(2)}) collective-permute-start(f32[32,1,8,128]{3,2,1,0:T(8,128)S(1)} %get-tuple-element.39), channel_id=1, source_target_pairs={{16,0},{32,16},{48,32},{64,48},{80,64},{96,80},{112,96},{128,112},... | collective-permute-start | bytes 393224 | tf_op jit(solution)/shard_map/ppermute | solution.py:32
  140.9 5.1 %collective-permute-start.8 = (f32[32,10,1,128]{3,0,2,1:T(8,128)S(1)}, f32[32,10,1,128]{3,0,2,1:T(8,128)S(1)}, u32[]{:S(2)}, u32[]{:S(2)}) collective-permute-start(f32[32,10,1,128]{3,0,2,1:T(8,128)S(1)} %copy.233), channel_id=1, source_target_pairs={{0,1},{1,2},{2,3},{3,4},{4,5},{5,6},{6,7},{7,8},{8,9},{9,10},{10,1... | collective-permute-start | bytes 491528 | tf_op jit(solution)/shard_map/ppermute | solution.py:29
  143.8 6.6 %collective-permute-start.9 = (f32[32,10,1,128]{3,0,2,1:T(8,128)S(1)}, f32[32,10,1,128]{3,0,2,1:T(8,128)S(1)}, u32[]{:S(2)}, u32[]{:S(2)}) collective-permute-start(f32[32,10,1,128]{3,0,2,1:T(8,128)S(1)} %copy.234), channel_id=1, source_target_pairs={{1,0},{2,1},{3,2},{4,3},{5,4},{6,5},{7,6},{8,7},{9,8},{10,9},{11,1... | collective-permute-start | bytes 491528 | tf_op jit(solution)/shard_map/ppermute | solution.py:32
  152.8 3.9 copy-start.3
  163.2 19.0 %copy-start.9 = (s32[8]{0:T(128)S(1)}, s32[8]{0:T(128)}, u32[]{:S(2)}) copy-start(s32[8]{0:T(128)} %reshape.107) | copy-start | bytes 100
  166.9 37.1 %copy-start.6 = (f32[256]{0:T(256)S(1)}, f32[256]{0:T(256)}, u32[]{:S(2)}) copy-start(f32[256]{0:T(256)} %param.11) | copy-start | bytes 3076
  175.6 18.4 %all-to-all-start.2 = ((f32[32,16,128]{2,0,1:T(8,128)}), f32[32,16,128]{2,0,1:T(8,128)S(1)}, u32[]{:S(2)}, u32[]{:S(2)}) async-start(f32[32,16,128]{2,0,1:T(8,128)} %copy.213), calls=%async_computation.2 | async-start | bytes 524288 | tf_op jit(solution)/shard_map/all_to_all | solution.py:152
  301.0 6.3 %collective-permute-start.10 = (f32[32,256]{0,1:T(8,128)S(1)}, f32[32,256]{0,1:T(8,128)S(1)}, u32[]{:S(2)}, u32[]{:S(2)}) collective-permute-start(f32[32,256]{0,1:T(8,128)S(1)} %multiply_subtract_fusion), channel_id=1, source_target_pairs={{0,1},{1,2},{2,3},{3,4},{4,5},{5,6},{6,7},{7,8},{8,9},{9,10},{10,1... | collective-permute-start | bytes 98312 | tf_op jit(solution)/shard_map/ppermute | solution.py:29
  304.8 6.3 %collective-permute-start.11 = (f32[32,256]{0,1:T(8,128)S(1)}, f32[32,256]{0,1:T(8,128)S(1)}, u32[]{:S(2)}, u32[]{:S(2)}) collective-permute-start(f32[32,256]{0,1:T(8,128)S(1)} %multiply_subtract_fusion), channel_id=1, source_target_pairs={{1,0},{2,1},{3,2},{4,3},{5,4},{6,5},{7,6},{8,7},{9,8},{10,9},{11,1... | collective-permute-start | bytes 98312 | tf_op jit(solution)/shard_map/ppermute | solution.py:32
  307.3 100.7 %copy-start.5 = (f32[32,256]{1,0:T(8,128)}, f32[32,256]{1,0:T(8,128)S(1)}, u32[]{:S(2)}) copy-start(f32[32,256]{1,0:T(8,128)S(1)} %copy.224) | copy-start | bytes 98308
  (1 other events, 3.9 us)
where the time goes:
time: 409 us; the launch traced here: 408 us
  blocking collectives  191 us (47%)
  other arithmetic  87.5 us (21%)
  starting transfers between devices  63.6 us (16%)
  waiting for transfers between devices  34.2 us (8%)
  local copies, waits for them, and re-layouts  27.8 us (7%)
    psum x1, blocking collectives, body(): lax.psum((jnp.sum(block_vectors * stiff_image, axis=1), jnp.sum(block_vec...  96.8 us
    psum x1, blocking collectives, body(): lax.psum((inner(search, image), inner(search, search)), ('passage', 'sub'))  94.6 us
    add x1, other arithmetic, pressure_solve(): second = first + second_step  23.2 us
    ppermute x6, starting transfers between devices, padded_2(): lax.ppermute(lax.slice_in_dim(block, 0, width, axis=dim), axis, backward)  21.9 us
    ppermute x6, starting transfers between devices, padded_2(): lax.ppermute(lax.slice_in_dim(block, block.shape[dim] - width, None, axis...  16 us
    scatter-add x1, other arithmetic, body(): source = jnp.zeros((modes, CX * CY * CZ), jnp.float32).at[:, cells_in].ad...  15.5 us
    concatenate x4, other arithmetic, padded_2(): block = jnp.concatenate([low, block, high], axis=dim)  14.5 us
    ppermute x6, waiting for transfers between devices, padded_2(): lax.ppermute(lax.slice_in_dim(block, 0, width, axis=dim), axis, backward)  12.1 us
  transfers between devices with their start and end apart: 15, of which 8 were waited for; matrix products, arithmetic and copies ran while one was open for 18% of the time, Pallas kernels for 0%

commit v1 on v0

v1 whole, which is shorter than its diff:
```python
import functools

import jax
import jax.numpy as jnp
from jax import lax
from jax.experimental import pallas as pl
from jax.experimental.pallas import tpu as pltpu
from jax.sharding import PartitionSpec as P

MESH = pl.DeviceIdType.MESH
F32 = jnp.float32
BF16 = jnp.bfloat16
I32 = jnp.int32

M = 32
CX = 8
CY = 8
CZ = 128
CAP = 128
NSD = 256

center_weight = 15.0
lower_bound = 1.0 / 15.0
upper_bound = 17.0 / 15.0
middle = (upper_bound + lower_bound) / 2.0
radius = (upper_bound - lower_bound) / 2.0
sigma_ratio = middle / radius
first_rho = 1.0 / sigma_ratio
second_rho = 1.0 / (2.0 * sigma_ratio - first_rho)
third_rho = 1.0 / (2.0 * sigma_ratio - second_rho)
FIRST = 1.0 / (center_weight * middle)
GAIN_TWO = 2.0 * second_rho / radius / center_weight
GAIN_THREE = 2.0 * third_rho / radius / center_weight
STEP_ONE = second_rho * first_rho * FIRST + GAIN_TWO * (1.0 - 17.0 * FIRST)
STEP_T = GAIN_TWO * 2.0 * FIRST
ALPHA = FIRST + STEP_ONE + third_rho * second_rho * STEP_ONE + GAIN_THREE * (1.0 - 17.0 * (FIRST + STEP_ONE))
BETA = STEP_T + third_rho * second_rho * STEP_T + GAIN_THREE * (2.0 * (FIRST + STEP_ONE) - 17.0 * STEP_T)
GAMMA = GAIN_THREE * 2.0 * STEP_T


def iota(shape, dim):
    return lax.broadcasted_iota(I32, shape, dim)


def nn(left, right):
    return jnp.dot(left, right, preferred_element_type=F32)


def nt(left, right):
    return lax.dot_general(left, right, (((1,), (1,)), ((), ())), preferred_element_type=F32)


def two(x):
    high = x.astype(BF16)
    return high, (x - high.astype(F32)).astype(BF16)


def three(x):
    high, rest = x.astype(BF16), None
    rest = x - high.astype(F32)
    middle_part = rest.astype(BF16)
    return high, middle_part, (rest - middle_part.astype(F32)).astype(BF16)


def kernel(
    n_passage,
    n_sub,
    v_ref,
    stiff_ref,
    mass_ref,
    kb_ref,
    cols_ref,
    node_ref,
    owner_ref,
    cell_ref,
    weight_ref,
    live_ref,
    resid_ref,
    gs_ref,
    gp_ref,
    win_v,
    win_s,
    win_w,
    kbh,
    kbl,
    mt,
    mt_in,
    n2,
    out,
    inc,
    rhot,
    s,
    xl,
    xr,
    pp,
    qq,
    ysl,
    ysr,
    yl,
    yr,
    fp,
    ret,
    back,
    gbuf,
    grecv,
    part,
    precv,
    gfull,
    nb_send,
    nb_recv,
    mt_send,
    mt_recv,
    a_send,
    a_recv,
    x_send,
    x_recv,
    y_send,
    y_recv,
    b_send,
    b_recv,
    g_send,
    g_recv,
    p_send,
    p_recv,
    f_send,
    f_recv,
):
    chips = n_sub // 2
    ni = node_ref.shape[0] * 128
    nc = node_ref.shape[0]
    rows = 128 // n_sub
    myp = lax.axis_index("passage")
    me = lax.axis_index("sub")
    chip = me // 2
    left_p = lax.rem(myp + n_passage - 1, n_passage)
    right_p = lax.rem(myp + 1, n_passage)
    has_left = me > 0
    has_right = me < n_sub - 1

    def sub_copy(src, dst, send, recv, peer):
        return pltpu.make_async_remote_copy(
            src_ref=src, dst_ref=dst, send_sem=send, recv_sem=recv,
            device_id={"sub": peer}, device_id_type=MESH,
        )

    def passage_copy(src, dst, send, recv, peer):
        return pltpu.make_async_remote_copy(
            src_ref=src, dst_ref=dst, send_sem=send, recv_sem=recv,
            device_id={"passage": peer}, device_id_type=MESH,
        )

    for win in (win_v, win_s, win_w):
        win[0:2] = jnp.zeros((2, M, 128), F32)
        win[4:6] = jnp.zeros((2, M, 128), F32)

    @pl.when(jnp.logical_not(has_left))
    def _():
        yl[...] = jnp.zeros_like(yl)

    @pl.when(jnp.logical_not(has_right))
    def _():
        yr[...] = jnp.zeros_like(yr)

    barrier = pltpu.get_barrier_semaphore()

    def greet_sub(i, carry):
        pl.semaphore_signal(barrier, inc=1, device_id={"sub": lax.rem(me + i, n_sub)}, device_id_type=MESH)
        return carry

    def greet_passage(i, carry):
        pl.semaphore_signal(barrier, inc=1, device_id={"passage": lax.rem(myp + i, n_passage)}, device_id_type=MESH)
        return carry

    lax.fori_loop(1, n_sub, greet_sub, 0)
    lax.fori_loop(1, n_passage, greet_passage, 0)

    v = v_ref[...]
    win_v[2] = v[:, :128]
    win_v[3] = v[:, 128:]

    owner = owner_ref[...]
    lane_of_slot = iota((1, ni), 1)

    def flat(x):
        return jnp.concatenate([x[c : c + 1, :] for c in range(nc)], axis=1)

    group = iota((n_sub, 128), 0)
    hot = [(owner[c : c + 1, :] == group).astype(F32) for c in range(nc)]
    upper = (iota((128, 128), 0) < iota((128, 128), 1)).astype(F32).astype(BF16)
    before = nn(jnp.concatenate(hot, axis=0).astype(BF16), upper)
    ahead = jnp.zeros((n_sub, 1), F32)
    ranks = []
    for c in range(nc):
        ranks.append(jnp.sum(hot[c] * (before[c * n_sub : (c + 1) * n_sub] + ahead), axis=0, keepdims=True))
        ahead = ahead + jnp.sum(hot[c], axis=1, keepdims=True)
    rank = jnp.concatenate(ranks, axis=1).astype(I32)
    rank_hot = (iota((CAP, ni), 0) == rank).astype(F32).astype(BF16)
    node = flat(node_ref[...]).astype(F32)
    cell = flat(cell_ref[...])
    weight = jnp.where(lane_of_slot < live_ref[0], flat(weight_ref[...]), 0.0)
    w0, w1, w2 = three(weight)
    which = iota((8, ni), 0)
    meta = jnp.zeros((8, ni), F32)
    for row, values in enumerate(
        (((cell >> 7) << 7).astype(F32), (cell & 127).astype(F32), node, w0.astype(F32), w1.astype(F32), w2.astype(F32))
    ):
        meta = jnp.where(which == row, values, meta)
    owner_row = flat(owner)
    lhs = jnp.concatenate([jnp.where(owner_row == g, meta, 0.0) for g in range(n_sub)], axis=0).astype(BF16)
    placed = nt(lhs, rank_hot)
    for g in range(n_sub):
        mt[g] = placed[g * 8 : (g + 1) * 8]

    pl.semaphore_wait(barrier, n_sub - 1 + n_passage - 1)

    def exchange(win, k):
        to_right = sub_copy(win.at[pl.ds(2, 2)], win.at[pl.ds(0, 2)], nb_send.at[k, 0], nb_recv.at[k, 0], me + 1)
        to_left = sub_copy(win.at[pl.ds(2, 2)], win.at[pl.ds(4, 2)], nb_send.at[k, 1], nb_recv.at[k, 1], me - 1)

        def start():
            pl.when(has_right)(to_right.start)
            pl.when(has_left)(to_left.start)

        def arrive():
            pl.when(has_left)(to_right.wait_recv)
            pl.when(has_right)(to_left.wait_recv)

        def sent():
            pl.when(has_right)(to_right.wait_send)
            pl.when(has_left)(to_left.wait_send)

        return start, arrive, sent

    v_start, v_arrive, v_sent = exchange(win_v, 0)
    s_start, s_arrive, s_sent = exchange(win_s, 1)
    w_start, w_arrive, w_sent = exchange(win_w, 2)

    def meta_copy(peer, slot):
        return sub_copy(mt.at[peer], mt_in.at[slot], mt_send.at[peer], mt_recv.at[slot], peer)

    def out_copy(peer, slot):
        return sub_copy(out.at[peer], inc.at[slot], a_send.at[peer], a_recv.at[slot], peer)

    def back_copy(peer, slot):
        return sub_copy(ret.at[peer], back.at[slot], b_send.at[peer], b_recv.at[slot], peer)

    def gram_copy(peer, slot):
        return sub_copy(gbuf.at[peer], grecv.at[slot], g_send.at[peer], g_recv.at[slot], peer)

    def full_copy(peer, slot):
        return sub_copy(part.at[1], gfull.at[slot], f_send.at[peer], f_recv.at[slot], peer)

    def part_copy(peer, slot):
        return passage_copy(part.at[0], precv.at[slot], p_send.at[peer], p_recv.at[slot], peer)

    def each_sub(act):
        def step(i, carry):
            act(lax.rem(me + i, n_sub))
            return carry

        lax.fori_loop(1, n_sub, step, 0)

    def each_passage(act):
        def step(i, carry):
            act(lax.rem(myp + i, n_passage))
            return carry

        lax.fori_loop(1, n_passage, step, 0)

    each_sub(lambda peer: meta_copy(peer, me).start())
    v_start()

    v3 = jnp.concatenate(three(v), axis=0)
    node_of = iota((NSD, 128), 0)

    def weight_row(g):
        return mt[g, 3:4, :] + mt[g, 4:5, :] + mt[g, 5:6, :]

    def send_step(t, carry):
        there = lax.rem(chip + 1 + t, chips)
        parts = [(node_of == mt[2 * there + core, 2:3, :].astype(I32)).astype(F32) for core in range(2)]
        one_hot = jnp.concatenate(parts, axis=1).astype(BF16)
        n2[there] = one_hot
        picked = nn(v3, one_hot)
        picked = picked[0:M] + picked[M : 2 * M] + picked[2 * M :]
        for core in range(2):
            g = 2 * there + core
            out[g] = picked[:, core * 128 : (core + 1) * 128] * weight_row(g)
            pl.when(g != me)(out_copy(g, me).start)
        return carry

    lax.fori_loop(0, chips, send_step, 0)
    inc[me] = out[me]
    mt_in[me] = mt[me]

    for r in range(2):
        kb = kb_ref[r]
        high, low = two(kb)
        kbh[r] = high
        kbl[r] = low

    stiff = stiff_ref[...]

    def apply(win, own):
        mixed = []
        for r in range(2):
            blocks = jnp.concatenate([win[cols_ref[r, n]] for n in range(4)], axis=1)
            high, low = two(blocks)
            both = nn(jnp.concatenate([high, low], axis=0), kbh[r])
            mixed.append(both[:M] + both[M:] + nn(high, kbl[r]))
        return stiff * own + jnp.concatenate(mixed, axis=1)

    v_arrive()
    image = apply(win_v, v)
    win_s[2] = image[:, :128]
    win_s[3] = image[:, 128:]
    s_start()

    s[...] = jnp.zeros_like(s)
    place = iota((512, 256), 0)

    def rows_of(there):
        high = jnp.concatenate([mt_in[2 * there + core, 0:1, :] for core in range(2)], axis=1).astype(I32)
        low = jnp.concatenate([mt_in[2 * there + core, 1:2, :] for core in range(2)], axis=1).astype(I32)
        return high >> 9, (high & 511) + low

    def take_step(t, carry):
        there = lax.rem(chip + chips - 1 - t + chips, chips)
        for core in range(2):
            j = 2 * there + core

            @pl.when(j != me)
            def _():
                meta_copy(j, j).wait_recv()
                out_copy(j, j).wait_recv()

        row, column = rows_of(there)
        one_hot = (place == column).astype(F32).astype(BF16)
        rhot[there] = one_hot
        values = jnp.concatenate([inc[2 * there], inc[2 * there + 1]], axis=1)
        high, low = two(values)
        for half in range(2):
            terms = []
            for k in range(8):
                mask = jnp.broadcast_to((row == half * 8 + k).astype(F32), (M, 256)).astype(BF16)
                terms.append(high * mask)
                terms.append(low * mask)
            product = nt(jnp.concatenate(terms, axis=0), one_hot)
            for k in range(8):
                term = product[k * 64 : k * 64 + 32] + product[k * 64 + 32 : k * 64 + 64]
                for q in range(4):
                    a, b = half * 4 + k // 2, (k % 2) * 4 + q
                    s[a, b] += term[:, q * 128 : (q + 1) * 128]
        return carry

    lax.fori_loop(0, chips, take_step, 0)

    x_right = passage_copy(s.at[pl.ds(6, 2)], xl, x_send.at[0], x_recv.at[0], right_p)
    x_left = passage_copy(s.at[pl.ds(0, 2)], xr, x_send.at[1], x_recv.at[1], left_p)
    x_right.start()
    x_left.start()

    s_arrive()
    image_image = apply(win_s, image)

    lane = iota((M, 128), 1)
    inner_low = (lane > 0).astype(F32) * 0.5
    inner_high = (lane < 127).astype(F32) * 0.5

    def along(x):
        return x + pltpu.roll(x, 1, 1) * inner_low + pltpu.roll(x, 127, 1) * inner_high

    def layer(a, b):
        if a < 0:
            return xl[a + 2, b]
        if a >= CX:
            return xr[a - CX, b]
        return s[a, b]

    def filters(layers):
        def step(b, carry):
            for a in layers:
                near = layer(a - 1, b) + layer(a + 1, b)
                mine = layer(a, b)
                far = layer(a - 2, b) + layer(a + 2, b)
                pp[a, b] = BETA * along(mine + 0.5 * near)
                qq[a, b] = GAMMA * along(along(1.5 * mine + near + 0.25 * far))
            return carry

        lax.fori_loop(0, CY, step, 0)

    filters((2, 3, 4, 5))
    x_right.wait_recv()
    x_left.wait_recv()
    filters((0, 1, 6, 7))

    def edge_step(a, carry):
        ysr[0, a] = 0.5 * pp[a, 7] + 0.25 * qq[a, 6] + qq[a, 7]
        ysr[1, a] = 0.25 * qq[a, 7]
        ysl[0, a] = 0.5 * pp[a, 0] + 0.25 * qq[a, 1] + qq[a, 0]
        ysl[1, a] = 0.25 * qq[a, 0]
        return carry

    lax.fori_loop(0, CX, edge_step, 0)
    y_right = sub_copy(ysr, yl, y_send.at[0], y_recv.at[0], me + 1)
    y_left = sub_copy(ysl, yr, y_send.at[1], y_recv.at[1], me - 1)
    pl.when(has_right)(y_right.start)
    pl.when(has_left)(y_left.start)
    pl.when(has_left)(y_right.wait_recv)
    pl.when(has_right)(y_left.wait_recv)
    end_left = jnp.where(has_left, 1.5, 1.25).astype(F32)
    end_right = jnp.where(has_right, 1.5, 1.25).astype(F32)

    def press_step(a, carry):
        p = [pp[a, b] for b in range(CY)]
        q = [qq[a, b] for b in range(CY)]
        for b in range(CY):
            near_p = [p[k] for k in (b - 1, b + 1) if 0 <= k < CY]
            near_q = [q[k] for k in (b - 1, b + 1) if 0 <= k < CY]
            far_q = [q[k] for k in (b - 2, b + 2) if 0 <= k < CY]
            centre = end_left if b == 0 else end_right if b == CY - 1 else 1.5
            total = ALPHA * s[a, b] + p[b] + 0.5 * sum(near_p) + centre * q[b] + sum(near_q) + 0.25 * sum(far_q)
            if b < 2:
                total = total + yl[b, a]
            if b >= CY - 2:
                total = total + yr[CY - 1 - b, a]
            high, low = two(total)
            fp[0, 2 * a + b // 4, :, (b % 4) * 128 : (b % 4 + 1) * 128] = high
            fp[1, 2 * a + b // 4, :, (b % 4) * 128 : (b % 4 + 1) * 128] = low
        return carry

    lax.fori_loop(0, CX, press_step, 0)

    def give_step(t, carry):
        there = lax.rem(chip + 1 + t, chips)
        row, _ = rows_of(there)
        one_hot = rhot[there]
        total = jnp.zeros((M, 256), F32)
        for half in range(2):
            product = nn(fp[0, half * 8 : half * 8 + 8].reshape(8 * M, 512), one_hot) + nn(
                fp[1, half * 8 : half * 8 + 8].reshape(8 * M, 512), one_hot
            )
            for k in range(8):
                total = total + jnp.where(row == half * 8 + k, product[k * M : (k + 1) * M], 0.0)
        for core in range(2):
            j = 2 * there + core
            ret[j] = total[:, core * 128 : (core + 1) * 128]
            pl.when(j != me)(back_copy(j, me).start)
        return carry

    lax.fori_loop(0, chips, give_step, 0)
    back[me] = ret[me]

    def force_step(t, total):
        there = lax.rem(chip + chips - 1 - t + chips, chips)
        for core in range(2):
            j = 2 * there + core

            @pl.when(j != me)
            def _():
                back_copy(j, j).wait_recv()

        forces = jnp.concatenate([back[2 * there + core] * weight_row(2 * there + core) for core in range(2)], axis=1)
        product = nt(jnp.concatenate(three(forces), axis=0), n2[there])
        return total + product[0:M] + product[M : 2 * M] + product[2 * M :]

    massed = lax.fori_loop(0, chips, force_step, mass_ref[...] * v)
    win_w[2] = massed[:, :128]
    win_w[3] = massed[:, 128:]
    w_start()
    w_arrive()
    image_massed = apply(win_w, massed)

    x_high, x_low = two(jnp.concatenate([v, image, massed], axis=0))
    z_high, z_low = two(
        jnp.concatenate([image, massed, image_image, image_massed, v, jnp.zeros((96, NSD), F32)], axis=0)
    )
    x_both = jnp.concatenate([x_high, x_low], axis=0)
    product = nt(x_both, z_high) + nt(x_both, z_low)
    product = product[:96] + product[96:]
    third = jnp.where(lane < M, product[0:32, 128:], product[64:96, :128])
    gram = jnp.concatenate([product[0:64, :128], third, jnp.zeros((32, 128), F32)], axis=0)
    for g in range(n_sub):
        gbuf[g] = gram[g * rows : (g + 1) * rows]
    each_sub(lambda peer: gram_copy(peer, me).start())
    grecv[me] = gbuf[me]
    each_sub(lambda peer: gram_copy(peer, peer).wait_recv())
    part[0] = lax.fori_loop(1, n_sub, lambda g, total: total + grecv[g], grecv[0])
    each_passage(lambda peer: part_copy(peer, myp).start())
    precv[myp] = part[0]
    each_passage(lambda peer: part_copy(peer, peer).wait_recv())
    part[1] = lax.fori_loop(1, n_passage, lambda g, total: total + precv[g], precv[0])
    each_sub(lambda peer: full_copy(peer, me).start())
    gfull[me] = part[1]
    each_sub(lambda peer: full_copy(peer, peer).wait_recv())

    whole = jnp.concatenate([gfull[g] for g in range(n_sub)], axis=0)
    turned = whole.T
    scale = 1.0 / (NSD * n_sub * n_passage)
    row_of = iota((M, 128), 0)

    def moved(x, blocks):
        return pltpu.roll(x, (128 - 32 * blocks) % 128, 1)

    top, mid, bottom = whole[0:32], whole[32:64], whole[64:96]
    numer = jnp.where(lane == row_of, top, 0.0)
    denom = jnp.where(lane == row_of, moved(top, 1), 0.0)
    theta = jnp.sum(numer, axis=1, keepdims=True) / jnp.sum(denom, axis=1, keepdims=True)
    theta_row = jnp.sum(jnp.where(lane == row_of, theta, 0.0), axis=0, keepdims=True)
    resid_ref[...] = image - theta * massed
    mass_stiff = moved(turned[32:64], 1)
    plain_vr = top - moved(top, 1) * theta_row
    plain_rv = turned[0:32] - theta * turned[32:64]
    stiff_rs = mid - theta * mass_stiff
    plain_rr = stiff_rs - moved(mid, 1) * theta_row + theta * theta_row * moved(bottom, 1)
    stiff_vr = moved(top, 2) - moved(top, 3) * theta_row
    stiff_rr = (
        moved(mid, 2) - theta * moved(bottom, 2) - moved(mid, 3) * theta_row + theta * theta_row * moved(bottom, 3)
    )

    def side(first, second):
        return (jnp.where(lane < M, first, pltpu.roll(second, 32, 1)) * scale)[:, : 2 * M]

    gs_ref[0:M, :] = side(top, stiff_vr)
    gs_ref[M:, :] = side(stiff_rs, stiff_rr)
    gp_ref[0:M, :] = side(bottom, plain_vr)
    gp_ref[M:, :] = side(plain_rv, plain_rr)

    each_sub(lambda peer: meta_copy(peer, me).wait_send())
    each_sub(lambda peer: out_copy(peer, me).wait_send())
    each_sub(lambda peer: back_copy(peer, me).wait_send())
    each_sub(lambda peer: gram_copy(peer, me).wait_send())
    each_sub(lambda peer: full_copy(peer, me).wait_send())
    each_passage(lambda peer: part_copy(peer, myp).wait_send())
    x_right.wait_send()
    x_left.wait_send()
    pl.when(has_right)(y_right.wait_send)
    pl.when(has_left)(y_left.wait_send)
    v_sent()
    s_sent()
    w_sent()


def body(
    n_passage,
    n_sub,
    block_vectors,
    stiffness,
    mass_diag,
    kblocks,
    block_cols,
    slot_node,
    slot_owner,
    slot_cell,
    slot_weight,
    live_slots,
):
    nc = slot_node.shape[0] // 128
    chips = n_sub // 2
    rows = 128 // n_sub
    vmem = pl.BlockSpec(memory_space=pltpu.VMEM)
    smem = pl.BlockSpec(memory_space=pltpu.SMEM)
    dma = pltpu.SemaphoreType.DMA
    layers = (2, CY, M, CZ)
    return pl.pallas_call(
        functools.partial(kernel, n_passage, n_sub),
        out_shape=(
            jax.ShapeDtypeStruct((M, NSD), F32),
            jax.ShapeDtypeStruct((2 * M, 2 * M), F32),
            jax.ShapeDtypeStruct((2 * M, 2 * M), F32),
        ),
        in_specs=[vmem, vmem, vmem, vmem, smem, vmem, vmem, vmem, vmem, smem],
        out_specs=(vmem, vmem, vmem),
        scratch_shapes=[
            pltpu.VMEM((6, M, 128), F32),
            pltpu.VMEM((6, M, 128), F32),
            pltpu.VMEM((6, M, 128), F32),
            pltpu.VMEM((2, 512, 128), BF16),
            pltpu.VMEM((2, 512, 128), BF16),
            pltpu.VMEM((n_sub, 8, 128), F32),
            pltpu.VMEM((n_sub, 8, 128), F32),
            pltpu.VMEM((chips, NSD, 256), BF16),
            pltpu.VMEM((n_sub, M, CAP), F32),
            pltpu.VMEM((n_sub, M, CAP), F32),
            pltpu.VMEM((chips, 512, 256), BF16),
            pltpu.VMEM((CX, CY, M, CZ), F32),
            pltpu.VMEM(layers, F32),
            pltpu.VMEM(layers, F32),
            pltpu.VMEM((CX, CY, M, CZ), F32),
            pltpu.VMEM((CX, CY, M, CZ), F32),
            pltpu.VMEM(layers, F32),
            pltpu.VMEM(layers, F32),
            pltpu.VMEM(layers, F32),
            pltpu.VMEM(layers, F32),
            pltpu.VMEM((2, 16, M, 512), BF16),
            pltpu.VMEM((n_sub, M, CAP), F32),
            pltpu.VMEM((n_sub, M, CAP), F32),
            pltpu.VMEM((n_sub, rows, 128), F32),
            pltpu.VMEM((n_sub, rows, 128), F32),
            pltpu.VMEM((2, rows, 128), F32),
            pltpu.VMEM((n_passage, rows, 128), F32),
            pltpu.VMEM((n_sub, rows, 128), F32),
            dma((3, 2)),
            dma((3, 2)),
            dma((n_sub,)),
            dma((n_sub,)),
            dma((n_sub,)),
            dma((n_sub,)),
            dma((2,)),
            dma((2,)),
            dma((2,)),
            dma((2,)),
            dma((n_sub,)),
            dma((n_sub,)),
            dma((n_sub,)),
            dma((n_sub,)),
            dma((n_passage,)),
            dma((n_passage,)),
            dma((n_sub,)),
            dma((n_sub,)),
        ],
        compiler_params=pltpu.CompilerParams(
            collective_id=0, has_side_effects=True, vmem_limit_bytes=48 * 1024 * 1024
        ),
    )(
        block_vectors,
        stiffness.reshape(1, NSD),
        mass_diag.reshape(1, NSD),
        kblocks.reshape(2, 512, 128),
        block_cols,
        slot_node.reshape(nc, 128),
        slot_owner.reshape(nc, 128),
        slot_cell.reshape(nc, 128),
        slot_weight.reshape(nc, 128),
        live_slots,
    )


def solution(mesh):
    return jax.shard_map(
        functools.partial(body, mesh.shape["passage"], mesh.shape["sub"]),
        mesh=mesh,
        in_specs=(
            P(None, ("passage", "sub")),
            P(("passage", "sub")),
            P(("passage", "sub")),
            P(("passage", "sub"), None, None, None),
            P(("passage", "sub"), None),
            P(("passage", "sub")),
            P(("passage", "sub"), None),
            P(("passage", "sub")),
            P(("passage", "sub")),
            P(("passage", "sub")),
        ),
        out_specs=(P(None, ("passage", "sub")), P(), P()),
        check_vma=False,
    )
```

time: 409 us -> 84.6 us (0.21)
  blocking collectives: 191 us -> 0 us
  other arithmetic: 87.5 us -> 0 us
  Pallas kernels: 0 us -> 77.9 us
  starting transfers between devices: 63.6 us -> 0 us
  waiting for transfers between devices: 34.2 us -> 0 us
  local copies, waits for them, and re-layouts: 27.8 us -> 5.01 us
    psum x2 -> x0, blocking collectives: 191 us -> none  [the longest x1 96.8 us: body(): lax.psum((jnp.sum(block_vectors * stiff_image, axis=1), jnp.sum(block_vec...]
    pallas_call x0 -> x1, Pallas kernels: none -> 77.9 us  [body(): pl.pallas_call(functools.partial(kernel, n_passage, n_sub), out_shape=(ja...]
    ppermute x12 -> x0, starting transfers between devices: 37.9 us -> none  [the longest x6 21.9 us: padded_2(): lax.ppermute(lax.slice_in_dim(block, 0, width, axis=dim), axis, backward)]
    add x3 -> x0, other arithmetic: 29.8 us -> none  [the longest x1 23.2 us: pressure_solve(): second = first + second_step]
    all_to_all x3 -> x0, starting transfers between devices: 25.7 us -> none  [the longest x1 11.8 us: body(): lax.all_to_all(cells_out, 'sub', split_axis=0, concat_axis=0, tiled=True)]
    scatter-add x2 -> x0, other arithmetic: 25.2 us -> none  [the longest x1 15.5 us: body(): source = jnp.zeros((modes, CX * CY * CZ), jnp.float32).at[:, cells_in].ad...]
    all_to_all x3 -> x0, waiting for transfers between devices: 21.4 us -> none  [the longest x1 11.7 us: body(): lax.all_to_all(outgoing, 'sub', split_axis=1, concat_axis=1, tiled=True)]
    concatenate x4 -> x0, other arithmetic: 14.5 us -> none  [padded_2(): block = jnp.concatenate([low, block, high], axis=dim)]
  transfers between devices with their start and end apart: 15 -> 0, of which waited for: 8 -> 0; matrix products, arithmetic and copies ran while one was open for 18% -> 0% of each run, Pallas kernels for 0% -> 0%
where the time goes in v1:
time: 84.6 us; the launch traced here: 84.3 us
  Pallas kernels  77.9 us (92%)
  local copies, waits for them, and re-layouts  5.01 us (6%)
  between operations  1.38 us (2%)
    pallas_call x1, Pallas kernels, body(): pl.pallas_call(functools.partial(kernel, n_passage, n_sub), out_shape=(ja...  77.9 us
    unnamed x21, local copies, waits for them, and re-layouts  5.01 us

profile of v1, /device:TPU:1, one launch (start us, length us, event | category | flops | bytes accessed | tf_op | source)
XLA Modules:
  0.0 84.3 jit_solution(3721302496519756263)
XLA Ops:
  0.6 0.0 copy-start.7
  0.6 0.0 copy-start.8
  1.3 0.0 copy-start.4
  1.3 0.0 copy-start.3
  1.3 0.0 copy-start.2
  1.3 0.0 copy-start.6
  1.4 0.0 copy-done.7
  1.4 0.0 copy-done.8
  1.4 0.6 copy-done.4
  2.0 0.0 copy-done.3
  2.0 0.0 copy-done.2
  2.0 0.0 copy-done.6
  2.0 0.0 copy-start
  2.0 1.0 %copy-done = f32[2,4,128,128]{3,2,1,0:T(8,128)S(1)} copy-done((f32[2,4,128,128]{3,2,1,0:T(8,128)S(1)}, f32[2,4,128,128]{3,2,1,0:T(8,128)}, u32[]{:S(2)}) %copy-start) | copy-done | bytes 524312
  3.1 0.0 copy-start.1
  3.1 0.8 copy-done.1
  3.8 0.0 copy-start.5
  3.8 0.7 copy-done.5
  4.5 77.9 %shard_map.121 = (f32[32,256]{1,0:T(8,128)S(1)}, f32[64,64]{1,0:T(8,128)S(1)}, f32[64,64]{1,0:T(8,128)S(1)}) custom-call(f32[32,256]{1,0:T(8,128)S(1)} %copy-done.1, f32[1,256]{1,0:T(1,128)S(1)} %bitcast.12, f32[1,256]{1,0:T(1,128)S(1)} %bitcast.13, f32[2,512,128]{2,1,0:T(8,128)S(1)} %bitcast.7, s32[2,4]{1,0:T(2,128)S(1)} %copy-done.8, ...), custom_call_target="tpu_custom_call" | custom-call | tf_op jit(solution)/shard_map/pallas_call | solution.py:565
  82.5 0.6 copy.17
  83.1 0.6 copy.18
  83.7 0.6 copy.19
Async XLA Ops:
  0.6 0.7 copy-start.7
  0.6 0.7 copy-start.8
  1.3 0.7 copy-start.4
  1.3 0.7 copy-start.3
  1.3 0.7 copy-start.2
  1.3 0.7 copy-start.6
  2.0 1.0 %copy-start = (f32[2,4,128,128]{3,2,1,0:T(8,128)S(1)}, f32[2,4,128,128]{3,2,1,0:T(8,128)}, u32[]{:S(2)}) copy-start(f32[2,4,128,128]{3,2,1,0:T(8,128)} %param.13) | copy-start | bytes 1572868
  3.1 0.8 copy-start.1
  3.8 0.7 copy-start.5

commit v2 on v1

--- a/solution.py
+++ b/solution.py
@@ -18,6 +18,8 @@
 CZ = 128
 CAP = 128
 NSD = 256
+CHUNKS = 2
+MC = M // CHUNKS
 
 center_weight = 15.0
 lower_bound = 1.0 / 15.0
@@ -65,6 +67,19 @@
 def kernel(
     n_passage,
     n_sub,
+    v_hbm,
+    stiff_hbm,
+    mass_hbm,
+    kb_hbm,
+    cols_hbm,
+    node_hbm,
+    owner_hbm,
+    cell_hbm,
+    weight_hbm,
+    live_hbm,
+    resid_ref,
+    gs_ref,
+    gp_ref,
     v_ref,
     stiff_ref,
     mass_ref,
@@ -75,16 +90,13 @@
     cell_ref,
     weight_ref,
     live_ref,
-    resid_ref,
-    gs_ref,
-    gp_ref,
+    in_sem,
     win_v,
     win_s,
     win_w,
     kbh,
     kbl,
     mt,
-    mt_in,
     n2,
     out,
     inc,
@@ -108,8 +120,6 @@
     gfull,
     nb_send,
     nb_recv,
-    mt_send,
-    mt_recv,
     a_send,
     a_recv,
     x_send,
@@ -149,6 +159,22 @@
             device_id={"passage": peer}, device_id_type=MESH,
         )
 
+    arguments = (
+        (node_hbm, node_ref),
+        (owner_hbm, owner_ref),
+        (cell_hbm, cell_ref),
+        (weight_hbm, weight_ref),
+        (live_hbm, live_ref),
+        (v_hbm, v_ref),
+        (kb_hbm, kb_ref),
+        (stiff_hbm, stiff_ref),
+        (mass_hbm, mass_ref),
+        (cols_hbm, cols_ref),
+    )
+    loads = [pltpu.make_async_copy(src, dst, in_sem.at[k]) for k, (src, dst) in enumerate(arguments)]
+    for load in loads:
+        load.start()
+
     for win in (win_v, win_s, win_w):
         win[0:2] = jnp.zeros((2, M, 128), F32)
         win[4:6] = jnp.zeros((2, M, 128), F32)
@@ -174,9 +200,8 @@
     lax.fori_loop(1, n_sub, greet_sub, 0)
     lax.fori_loop(1, n_passage, greet_passage, 0)
 
-    v = v_ref[...]
-    win_v[2] = v[:, :128]
-    win_v[3] = v[:, 128:]
+    for load in loads[:5]:
+        load.wait()
 
     owner = owner_ref[...]
     lane_of_slot = iota((1, ni), 1)
@@ -210,6 +235,11 @@
     placed = nt(lhs, rank_hot)
     for g in range(n_sub):
         mt[g] = placed[g * 8 : (g + 1) * 8]
+    for load in loads[5:]:
+        load.wait()
+    v = v_ref[...]
+    win_v[2] = v[:, :128]
+    win_v[3] = v[:, 128:]
 
     pl.semaphore_wait(barrier, n_sub - 1 + n_passage - 1)
 
@@ -235,14 +265,14 @@
     s_start, s_arrive, s_sent = exchange(win_s, 1)
     w_start, w_arrive, w_sent = exchange(win_w, 2)
 
-    def meta_copy(peer, slot):
-        return sub_copy(mt.at[peer], mt_in.at[slot], mt_send.at[peer], mt_recv.at[slot], peer)
-
-    def out_copy(peer, slot):
-        return sub_copy(out.at[peer], inc.at[slot], a_send.at[peer], a_recv.at[slot], peer)
-
-    def back_copy(peer, slot):
-        return sub_copy(ret.at[peer], back.at[slot], b_send.at[peer], b_recv.at[slot], peer)
+    def out_copy(c, peer, slot):
+        sent_rows = pl.ds(0, MC + 8 if c == 0 else MC)
+        return sub_copy(
+            out.at[c, peer, sent_rows], inc.at[c, slot, sent_rows], a_send.at[c, peer], a_recv.at[c, slot], peer
+        )
+
+    def back_copy(c, peer, slot):
+        return sub_copy(ret.at[c, peer], back.at[c, slot], b_send.at[c, peer], b_recv.at[c, slot], peer)
 
     def gram_copy(peer, slot):
         return sub_copy(gbuf.at[peer], grecv.at[slot], g_send.at[peer], g_recv.at[slot], peer)
@@ -267,8 +297,8 @@
 
         lax.fori_loop(1, n_passage, step, 0)
 
-    each_sub(lambda peer: meta_copy(peer, me).start())
     v_start()
+    departures = [v_sent]
 
     v3 = jnp.concatenate(three(v), axis=0)
     node_of = iota((NSD, 128), 0)
@@ -285,13 +315,19 @@
         picked = picked[0:M] + picked[M : 2 * M] + picked[2 * M :]
         for core in range(2):
             g = 2 * there + core
-            out[g] = picked[:, core * 128 : (core + 1) * 128] * weight_row(g)
-            pl.when(g != me)(out_copy(g, me).start)
+            values = picked[:, core * 128 : (core + 1) * 128] * weight_row(g)
+            for c in range(CHUNKS):
+                out[c, g, 0:MC, :] = values[c * MC : (c + 1) * MC]
+            out[0, g, MC : MC + 8, :] = mt[g]
+            pl.when(g != me)(out_copy(0, g, me).start)
         return carry
 
     lax.fori_loop(0, chips, send_step, 0)
-    inc[me] = out[me]
-    mt_in[me] = mt[me]
+    for c in range(1, CHUNKS):
+        each_sub(lambda peer, c=c: out_copy(c, peer, me).start())
+    for c in range(CHUNKS):
+        departures.append(lambda c=c: each_sub(lambda peer: out_copy(c, peer, me).wait_send()))
+        inc[c, me] = out[c, me]
 
     for r in range(2):
         kb = kb_ref[r]
@@ -315,159 +351,174 @@
     win_s[2] = image[:, :128]
     win_s[3] = image[:, 128:]
     s_start()
-
-    s[...] = jnp.zeros_like(s)
+    departures.append(s_sent)
+
     place = iota((512, 256), 0)
 
     def rows_of(there):
-        high = jnp.concatenate([mt_in[2 * there + core, 0:1, :] for core in range(2)], axis=1).astype(I32)
-        low = jnp.concatenate([mt_in[2 * there + core, 1:2, :] for core in range(2)], axis=1).astype(I32)
+        high = jnp.concatenate([inc[0, 2 * there + k, MC : MC + 1, :] for k in range(2)], axis=1).astype(I32)
+        low = jnp.concatenate([inc[0, 2 * there + k, MC + 1 : MC + 2, :] for k in range(2)], axis=1).astype(I32)
         return high >> 9, (high & 511) + low
 
-    def take_step(t, carry):
-        there = lax.rem(chip + chips - 1 - t + chips, chips)
+    def each_source(there, act):
         for core in range(2):
             j = 2 * there + core
-
-            @pl.when(j != me)
-            def _():
-                meta_copy(j, j).wait_recv()
-                out_copy(j, j).wait_recv()
-
-        row, column = rows_of(there)
-        one_hot = (place == column).astype(F32).astype(BF16)
-        rhot[there] = one_hot
-        values = jnp.concatenate([inc[2 * there], inc[2 * there + 1]], axis=1)
-        high, low = two(values)
-        for half in range(2):
+            pl.when(j != me)(functools.partial(act, j))
+
+    def take(c):
+        s[c] = jnp.zeros((CX, CY, MC, CZ), F32)
+
+        def step(t, carry):
+            there = lax.rem(chip + 2 * chips - 1 - t, chips)
+            each_source(there, lambda j: out_copy(c, j, j).wait_recv())
+            row, column = rows_of(there)
+            if c == 0:
+                one_hot = (place == column).astype(F32).astype(BF16)
+                rhot[there] = one_hot
+            else:
+                one_hot = rhot[there]
+            values = jnp.concatenate([inc[c, 2 * there, 0:MC, :], inc[c, 2 * there + 1, 0:MC, :]], axis=1)
+            high, low = two(values)
             terms = []
-            for k in range(8):
-                mask = jnp.broadcast_to((row == half * 8 + k).astype(F32), (M, 256)).astype(BF16)
+            for k in range(16):
+                mask = jnp.broadcast_to((row == k).astype(F32), (MC, 256)).astype(BF16)
                 terms.append(high * mask)
                 terms.append(low * mask)
             product = nt(jnp.concatenate(terms, axis=0), one_hot)
-            for k in range(8):
-                term = product[k * 64 : k * 64 + 32] + product[k * 64 + 32 : k * 64 + 64]
+            for k in range(16):
+                term = product[2 * k * MC : (2 * k + 1) * MC] + product[(2 * k + 1) * MC : (2 * k + 2) * MC]
                 for q in range(4):
-                    a, b = half * 4 + k // 2, (k % 2) * 4 + q
-                    s[a, b] += term[:, q * 128 : (q + 1) * 128]
-        return carry
-
-    lax.fori_loop(0, chips, take_step, 0)
-
-    x_right = passage_copy(s.at[pl.ds(6, 2)], xl, x_send.at[0], x_recv.at[0], right_p)
-    x_left = passage_copy(s.at[pl.ds(0, 2)], xr, x_send.at[1], x_recv.at[1], left_p)
-    x_right.start()
-    x_left.start()
+                    s[c, k // 2, (k % 2) * 4 + q] += term[:, q * 128 : (q + 1) * 128]
+            return carry
+
+        lax.fori_loop(0, chips, step, 0)
+
+    x_right = [
+        passage_copy(s.at[c, pl.ds(6, 2)], xl.at[c], x_send.at[c, 0], x_recv.at[c, 0], right_p) for c in range(CHUNKS)
+    ]
+    x_left = [
+        passage_copy(s.at[c, pl.ds(0, 2)], xr.at[c], x_send.at[c, 1], x_recv.at[c, 1], left_p) for c in range(CHUNKS)
+    ]
+    for c in range(CHUNKS):
+        take(c)
+        x_right[c].start()
+        x_left[c].start()
+        departures += [x_right[c].wait_send, x_left[c].wait_send]
 
     s_arrive()
     image_image = apply(win_s, image)
 
     lane = iota((M, 128), 1)
-    inner_low = (lane > 0).astype(F32) * 0.5
-    inner_high = (lane < 127).astype(F32) * 0.5
+    chunk_lane = iota((MC, 128), 1)
+    inner_low = (chunk_lane > 0).astype(F32) * 0.5
+    inner_high = (chunk_lane < 127).astype(F32) * 0.5
 
     def along(x):
         return x + pltpu.roll(x, 1, 1) * inner_low + pltpu.roll(x, 127, 1) * inner_high
 
-    def layer(a, b):
-        if a < 0:
-            return xl[a + 2, b]
-        if a >= CX:
-            return xr[a - CX, b]
-        return s[a, b]
-
-    def filters(layers):
+    def filters(c, layers):
+        def layer(a, b):
+            if a < 0:
+                return xl[c, a + 2, b]
+            if a >= CX:
+                return xr[c, a - CX, b]
+            return s[c, a, b]
+
         def step(b, carry):
             for a in layers:
                 near = layer(a - 1, b) + layer(a + 1, b)
                 mine = layer(a, b)
                 far = layer(a - 2, b) + layer(a + 2, b)
-                pp[a, b] = BETA * along(mine + 0.5 * near)
-                qq[a, b] = GAMMA * along(along(1.5 * mine + near + 0.25 * far))
+                pp[c, a, b] = BETA * along(mine + 0.5 * near)
+                qq[c, a, b] = GAMMA * along(along(1.5 * mine + near + 0.25 * far))
             return carry
 
         lax.fori_loop(0, CY, step, 0)
 
-    filters((2, 3, 4, 5))
-    x_right.wait_recv()
-    x_left.wait_recv()
-    filters((0, 1, 6, 7))
-
-    def edge_step(a, carry):
-        ysr[0, a] = 0.5 * pp[a, 7] + 0.25 * qq[a, 6] + qq[a, 7]
-        ysr[1, a] = 0.25 * qq[a, 7]
-        ysl[0, a] = 0.5 * pp[a, 0] + 0.25 * qq[a, 1] + qq[a, 0]
-        ysl[1, a] = 0.25 * qq[a, 0]
-        return carry
-
-    lax.fori_loop(0, CX, edge_step, 0)
-    y_right = sub_copy(ysr, yl, y_send.at[0], y_recv.at[0], me + 1)
-    y_left = sub_copy(ysl, yr, y_send.at[1], y_recv.at[1], me - 1)
-    pl.when(has_right)(y_right.start)
-    pl.when(has_left)(y_left.start)
-    pl.when(has_left)(y_right.wait_recv)
-    pl.when(has_right)(y_left.wait_recv)
+    y_right = [sub_copy(ysr.at[c], yl.at[c], y_send.at[c, 0], y_recv.at[c, 0], me + 1) for c in range(CHUNKS)]
+    y_left = [sub_copy(ysl.at[c], yr.at[c], y_send.at[c, 1], y_recv.at[c, 1], me - 1) for c in range(CHUNKS)]
+    for c in range(CHUNKS):
+        filters(c, (2, 3, 4, 5))
+        x_right[c].wait_recv()
+        x_left[c].wait_recv()
+        filters(c, (0, 1, 6, 7))
+
+        def edge_step(a, carry):
+            ysr[c, 0, a] = 0.5 * pp[c, a, 7] + 0.25 * qq[c, a, 6] + qq[c, a, 7]
+            ysr[c, 1, a] = 0.25 * qq[c, a, 7]
+            ysl[c, 0, a] = 0.5 * pp[c, a, 0] + 0.25 * qq[c, a, 1] + qq[c, a, 0]
+            ysl[c, 1, a] = 0.25 * qq[c, a, 0]
+            return carry
+
+        lax.fori_loop(0, CX, edge_step, 0)
+        pl.when(has_right)(y_right[c].start)
+        pl.when(has_left)(y_left[c].start)
+        departures.append(lambda c=c: pl.when(has_right)(y_right[c].wait_send))
+        departures.append(lambda c=c: pl.when(has_left)(y_left[c].wait_send))
+
     end_left = jnp.where(has_left, 1.5, 1.25).astype(F32)
     end_right = jnp.where(has_right, 1.5, 1.25).astype(F32)
 
-    def press_step(a, carry):
-        p = [pp[a, b] for b in range(CY)]
-        q = [qq[a, b] for b in range(CY)]
-        for b in range(CY):
-            near_p = [p[k] for k in (b - 1, b + 1) if 0 <= k < CY]
-            near_q = [q[k] for k in (b - 1, b + 1) if 0 <= k < CY]
-            far_q = [q[k] for k in (b - 2, b + 2) if 0 <= k < CY]
-            centre = end_left if b == 0 else end_right if b == CY - 1 else 1.5
-            total = ALPHA * s[a, b] + p[b] + 0.5 * sum(near_p) + centre * q[b] + sum(near_q) + 0.25 * sum(far_q)
-            if b < 2:
-                total = total + yl[b, a]
-            if b >= CY - 2:
-                total = total + yr[CY - 1 - b, a]
-            high, low = two(total)
-            fp[0, 2 * a + b // 4, :, (b % 4) * 128 : (b % 4 + 1) * 128] = high
-            fp[1, 2 * a + b // 4, :, (b % 4) * 128 : (b % 4 + 1) * 128] = low
-        return carry
-
-    lax.fori_loop(0, CX, press_step, 0)
-
-    def give_step(t, carry):
-        there = lax.rem(chip + 1 + t, chips)
-        row, _ = rows_of(there)
-        one_hot = rhot[there]
-        total = jnp.zeros((M, 256), F32)
-        for half in range(2):
-            product = nn(fp[0, half * 8 : half * 8 + 8].reshape(8 * M, 512), one_hot) + nn(
-                fp[1, half * 8 : half * 8 + 8].reshape(8 * M, 512), one_hot
-            )
-            for k in range(8):
-                total = total + jnp.where(row == half * 8 + k, product[k * M : (k + 1) * M], 0.0)
-        for core in range(2):
-            j = 2 * there + core
-            ret[j] = total[:, core * 128 : (core + 1) * 128]
-            pl.when(j != me)(back_copy(j, me).start)
-        return carry
-
-    lax.fori_loop(0, chips, give_step, 0)
-    back[me] = ret[me]
-
-    def force_step(t, total):
-        there = lax.rem(chip + chips - 1 - t + chips, chips)
-        for core in range(2):
-            j = 2 * there + core
-
-            @pl.when(j != me)
-            def _():
-                back_copy(j, j).wait_recv()
-
-        forces = jnp.concatenate([back[2 * there + core] * weight_row(2 * there + core) for core in range(2)], axis=1)
-        product = nt(jnp.concatenate(three(forces), axis=0), n2[there])
-        return total + product[0:M] + product[M : 2 * M] + product[2 * M :]
-
-    massed = lax.fori_loop(0, chips, force_step, mass_ref[...] * v)
+    def press(c):
+        def step(a, carry):
+            p = [pp[c, a, b] for b in range(CY)]
+            q = [qq[c, a, b] for b in range(CY)]
+            for b in range(CY):
+                near_p = [p[k] for k in (b - 1, b + 1) if 0 <= k < CY]
+                near_q = [q[k] for k in (b - 1, b + 1) if 0 <= k < CY]
+                far_q = [q[k] for k in (b - 2, b + 2) if 0 <= k < CY]
+                centre = end_left if b == 0 else end_right if b == CY - 1 else 1.5
+                total = ALPHA * s[c, a, b] + p[b] + 0.5 * sum(near_p) + centre * q[b] + sum(near_q) + 0.25 * sum(far_q)
+                if b < 2:
+                    total = total + yl[c, b, a]
+                if b >= CY - 2:
+                    total = total + yr[c, CY - 1 - b, a]
+                high, low = two(total)
+                fp[0, 2 * a + b // 4, :, (b % 4) * 128 : (b % 4 + 1) * 128] = high
+                fp[1, 2 * a + b // 4, :, (b % 4) * 128 : (b % 4 + 1) * 128] = low
+            return carry
+
+        lax.fori_loop(0, CX, step, 0)
+
+    def give(c):
+        def step(t, carry):
+            there = lax.rem(chip + 1 + t, chips)
+            row, _ = rows_of(there)
+            product = nn(fp[...].reshape(32 * MC, 512), rhot[there])
+            total = jnp.zeros((MC, 256), F32)
+            for k in range(16):
+                both = product[k * MC : (k + 1) * MC] + product[(16 + k) * MC : (17 + k) * MC]
+                total = total + jnp.where(row == k, both, 0.0)
+            for core in range(2):
+                ret[c, 2 * there + core] = total[:, core * 128 : (core + 1) * 128]
+            each_source(there, lambda j: back_copy(c, j, me).start())
+            return carry
+
+        lax.fori_loop(0, chips, step, 0)
+        back[c, me] = ret[c, me]
+
+    for c in range(CHUNKS):
+        pl.when(has_left)(y_right[c].wait_recv)
+        pl.when(has_right)(y_left[c].wait_recv)
+        press(c)
+        give(c)
+        departures.append(lambda c=c: each_sub(lambda peer: back_copy(c, peer, me).wait_send()))
+
+    def forces(c):
+        def step(t, total):
+            there = lax.rem(chip + 2 * chips - 1 - t, chips)
+            each_source(there, lambda j: back_copy(c, j, j).wait_recv())
+            force = jnp.concatenate([back[c, 2 * there + k] * weight_row(2 * there + k) for k in range(2)], axis=1)
+            product = nt(jnp.concatenate(three(force), axis=0), n2[there])
+            return total + product[0:MC] + product[MC : 2 * MC] + product[2 * MC :]
+
+        return lax.fori_loop(0, chips, step, mass_ref[...] * v[c * MC : (c + 1) * MC])
+
+    massed = jnp.concatenate([forces(c) for c in range(CHUNKS)], axis=0)
     win_w[2] = massed[:, :128]
     win_w[3] = massed[:, 128:]
     w_start()
+    departures.append(w_sent)
     w_arrive()
     image_massed = apply(win_w, massed)
 
@@ -483,14 +534,17 @@
     for g in range(n_sub):
         gbuf[g] = gram[g * rows : (g + 1) * rows]
     each_sub(lambda peer: gram_copy(peer, me).start())
+    departures.append(lambda: each_sub(lambda peer: gram_copy(peer, me).wait_send()))
     grecv[me] = gbuf[me]
     each_sub(lambda peer: gram_copy(peer, peer).wait_recv())
     part[0] = lax.fori_loop(1, n_sub, lambda g, total: total + grecv[g], grecv[0])
     each_passage(lambda peer: part_copy(peer, myp).start())
+    departures.append(lambda: each_passage(lambda peer: part_copy(peer, myp).wait_send()))
     precv[myp] = part[0]
     each_passage(lambda peer: part_copy(peer, peer).wait_recv())
     part[1] = lax.fori_loop(1, n_passage, lambda g, total: total + precv[g], precv[0])
     each_sub(lambda peer: full_copy(peer, me).start())
+    departures.append(lambda: each_sub(lambda peer: full_copy(peer, me).wait_send()))
     gfull[me] = part[1]
     each_sub(lambda peer: full_copy(peer, peer).wait_recv())
 
@@ -526,19 +580,8 @@
     gp_ref[0:M, :] = side(bottom, plain_vr)
     gp_ref[M:, :] = side(plain_rv, plain_rr)
 
-    each_sub(lambda peer: meta_copy(peer, me).wait_send())
-    each_sub(lambda peer: out_copy(peer, me).wait_send())
-    each_sub(lambda peer: back_copy(peer, me).wait_send())
-    each_sub(lambda peer: gram_copy(peer, me).wait_send())
-    each_sub(lambda peer: full_copy(peer, me).wait_send())
-    each_passage(lambda peer: part_copy(peer, myp).wait_send())
-    x_right.wait_send()
-    x_left.wait_send()
-    pl.when(has_right)(y_right.wait_send)
-    pl.when(has_left)(y_left.wait_send)
-    v_sent()
-    s_sent()
-    w_sent()
+    for sent in departures:
+        sent()
 
 
 def body(
@@ -559,9 +602,10 @@
     chips = n_sub // 2
     rows = 128 // n_sub
     vmem = pl.BlockSpec(memory_space=pltpu.VMEM)
-    smem = pl.BlockSpec(memory_space=pltpu.SMEM)
+    hbm = pl.BlockSpec(memory_space=pltpu.HBM)
     dma = pltpu.SemaphoreType.DMA
-    layers = (2, CY, M, CZ)
+    layers = pltpu.VMEM((CHUNKS, 2, CY, MC, CZ), F32)
+    cells = pltpu.VMEM((CHUNKS, CX, CY, MC, CZ), F32)
     return pl.pallas_call(
         functools.partial(kernel, n_passage, n_sub),
         out_shape=(
@@ -569,32 +613,42 @@
             jax.ShapeDtypeStruct((2 * M, 2 * M), F32),
             jax.ShapeDtypeStruct((2 * M, 2 * M), F32),
         ),
-        in_specs=[vmem, vmem, vmem, vmem, smem, vmem, vmem, vmem, vmem, smem],
+        in_specs=[hbm] * 10,
         out_specs=(vmem, vmem, vmem),
         scratch_shapes=[
+            pltpu.VMEM((M, NSD), F32),
+            pltpu.VMEM((1, NSD), F32),
+            pltpu.VMEM((1, NSD), F32),
+            pltpu.VMEM((2, 512, 128), F32),
+            pltpu.SMEM((2, 4), I32),
+            pltpu.VMEM((nc, 128), I32),
+            pltpu.VMEM((nc, 128), I32),
+            pltpu.VMEM((nc, 128), I32),
+            pltpu.VMEM((nc, 128), F32),
+            pltpu.SMEM((1,), I32),
+            dma((10,)),
             pltpu.VMEM((6, M, 128), F32),
             pltpu.VMEM((6, M, 128), F32),
             pltpu.VMEM((6, M, 128), F32),
             pltpu.VMEM((2, 512, 128), BF16),
             pltpu.VMEM((2, 512, 128), BF16),
             pltpu.VMEM((n_sub, 8, 128), F32),
-            pltpu.VMEM((n_sub, 8, 128), F32),
             pltpu.VMEM((chips, NSD, 256), BF16),
-            pltpu.VMEM((n_sub, M, CAP), F32),
-            pltpu.VMEM((n_sub, M, CAP), F32),
+            pltpu.VMEM((CHUNKS, n_sub, MC + 8, CAP), F32),
+            pltpu.VMEM((CHUNKS, n_sub, MC + 8, CAP), F32),
             pltpu.VMEM((chips, 512, 256), BF16),
-            pltpu.VMEM((CX, CY, M, CZ), F32),
-            pltpu.VMEM(layers, F32),
-            pltpu.VMEM(layers, F32),
-            pltpu.VMEM((CX, CY, M, CZ), F32),
-            pltpu.VMEM((CX, CY, M, CZ), F32),
-            pltpu.VMEM(layers, F32),
-            pltpu.VMEM(layers, F32),
-            pltpu.VMEM(layers, F32),
-            pltpu.VMEM(layers, F32),
-            pltpu.VMEM((2, 16, M, 512), BF16),
-            pltpu.VMEM((n_sub, M, CAP), F32),
-            pltpu.VMEM((n_sub, M, CAP), F32),
+            cells,
+            layers,
+            layers,
+            cells,
+            cells,
+            layers,
+            layers,
+            layers,
+            layers,
+            pltpu.VMEM((2, 16, MC, 512), BF16),
+            pltpu.VMEM((CHUNKS, n_sub, MC, CAP), F32),
+            pltpu.VMEM((CHUNKS, n_sub, MC, CAP), F32),
             pltpu.VMEM((n_sub, rows, 128), F32),
             pltpu.VMEM((n_sub, rows, 128), F32),
             pltpu.VMEM((2, rows, 128), F32),
@@ -602,16 +656,14 @@
             pltpu.VMEM((n_sub, rows, 128), F32),
             dma((3, 2)),
             dma((3, 2)),
-            dma((n_sub,)),
-            dma((n_sub,)),
-            dma((n_sub,)),
-            dma((n_sub,)),
-            dma((2,)),
-            dma((2,)),
-            dma((2,)),
-            dma((2,)),
-            dma((n_sub,)),
-            dma((n_sub,)),
+            dma((CHUNKS, n_sub)),
+            dma((CHUNKS, n_sub)),
+            dma((CHUNKS, 2)),
+            dma((CHUNKS, 2)),
+            dma((CHUNKS, 2)),
+            dma((CHUNKS, 2)),
+            dma((CHUNKS, n_sub)),
+            dma((CHUNKS, n_sub)),
             dma((n_sub,)),
             dma((n_sub,)),
             dma((n_passage,)),
@@ -620,7 +672,7 @@
             dma((n_sub,)),
         ],
         compiler_params=pltpu.CompilerParams(
-            collective_id=0, has_side_effects=True, vmem_limit_bytes=48 * 1024 * 1024
+            collective_id=0, has_side_effects=True, vmem_limit_bytes=60 * 1024 * 1024
         ),
     )(
         block_vectors,

time: 84.6 us -> 78.9 us (0.933)
  Pallas kernels: 77.9 us -> 74.5 us
  local copies, waits for them, and re-layouts: 5.01 us -> 2.77 us
    pallas_call x1, Pallas kernels: 77.9 us -> 74.5 us  [body(): pl.pallas_call(functools.partial(kernel, n_passage, n_sub), out_shape=(ja...]
    unnamed x21 -> x7, local copies, waits for them, and re-layouts: 5.01 us -> 2.77 us
where the time goes in v2:
time: 78.9 us; the launch traced here: 78.6 us
  Pallas kernels  74.5 us (94%)
  local copies, waits for them, and re-layouts  2.77 us (4%)
  between operations  1.3 us (2%)
    pallas_call x1, Pallas kernels, body(): pl.pallas_call(functools.partial(kernel, n_passage, n_sub), out_shape=(ja...  74.5 us
    unnamed x7, local copies, waits for them, and re-layouts  2.77 us

profile of v2, /device:TPU:1, one launch (start us, length us, event | category | flops | bytes accessed | tf_op | source)
XLA Modules:
  0.0 78.6 jit_solution(11485180566862377316)
XLA Ops:
  1.3 74.5 %shard_map.121 = (f32[32,256]{1,0:T(8,128)}, f32[64,64]{1,0:T(8,128)}, f32[64,64]{1,0:T(8,128)}) custom-call(f32[32,256]{1,0:T(8,128)} %v_hbm.1, f32[1,256]{1,0:T(1,128)} %bitcast.12, f32[1,256]{1,0:T(1,128)} %bitcast.13, f32[2,512,128]{2,1,0:T(8,128)} %bitcast.7, s32[2,4]{1,0:T(2,128)} %cols_hbm.1, s32[8,128]{1,0:T(8,128)} %bitcast.8, s32[8,128]{1,0:T(8,128)} %bitcast.9, ...), custom_call_target="tpu_custom_call" | custom-call | tf_op jit(solution)/shard_map/pallas_call | solution.py:609
  75.8 0.0 copy-start.1
  75.8 1.4 %copy.17 = f32[32,256]{1,0:T(8,128)} copy(f32[32,256]{1,0:T(8,128)} %get-tuple-element.6) | data formatting | bytes 65536
  77.2 0.0 copy-done.1
  77.2 0.0 copy-start
  77.2 0.6 copy.18
  77.8 0.2 copy-done
  78.0 0.6 copy.19
Async XLA Ops:
  75.8 1.4 %copy-start.1 = (f32[64,64]{1,0:T(8,128)S(1)}, f32[64,64]{1,0:T(8,128)}, u32[]{:S(2)}) copy-start(f32[64,64]{1,0:T(8,128)} %get-tuple-element.7) | copy-start | bytes 49156
  77.2 0.8 copy-start

commit v3 on v2

--- a/solution.py
+++ b/solution.py
@@ -118,6 +118,7 @@
     part,
     precv,
     gfull,
+    whole,
     nb_send,
     nb_recv,
     a_send,
@@ -138,7 +139,7 @@
     chips = n_sub // 2
     ni = node_ref.shape[0] * 128
     nc = node_ref.shape[0]
-    rows = 128 // n_sub
+    rows = 3 * M // n_sub
     myp = lax.axis_index("passage")
     me = lax.axis_index("sub")
     chip = me // 2
@@ -266,7 +267,7 @@
     w_start, w_arrive, w_sent = exchange(win_w, 2)
 
     def out_copy(c, peer, slot):
-        sent_rows = pl.ds(0, MC + 8 if c == 0 else MC)
+        sent_rows = pl.ds(0, MC + 2 if c == 0 else MC)
         return sub_copy(
             out.at[c, peer, sent_rows], inc.at[c, slot, sent_rows], a_send.at[c, peer], a_recv.at[c, slot], peer
         )
@@ -274,28 +275,40 @@
     def back_copy(c, peer, slot):
         return sub_copy(ret.at[c, peer], back.at[c, slot], b_send.at[c, peer], b_recv.at[c, slot], peer)
 
+    kept = pl.ds(0, rows)
+
     def gram_copy(peer, slot):
-        return sub_copy(gbuf.at[peer], grecv.at[slot], g_send.at[peer], g_recv.at[slot], peer)
+        return sub_copy(gbuf.at[peer, kept], grecv.at[slot, kept], g_send.at[peer], g_recv.at[slot], peer)
 
     def full_copy(peer, slot):
-        return sub_copy(part.at[1], gfull.at[slot], f_send.at[peer], f_recv.at[slot], peer)
+        return sub_copy(part.at[1, kept], gfull.at[slot, kept], f_send.at[peer], f_recv.at[slot], peer)
 
     def part_copy(peer, slot):
-        return passage_copy(part.at[0], precv.at[slot], p_send.at[peer], p_recv.at[slot], peer)
+        return passage_copy(part.at[0, kept], precv.at[slot, kept], p_send.at[peer], p_recv.at[slot], peer)
+
+    def far_first(k, count):
+        half = (k + 1) // 2
+        return count // 2 + jnp.where(lax.rem(k, 2) == 1, -half, half)
 
     def each_sub(act):
-        def step(i, carry):
-            act(lax.rem(me + i, n_sub))
+        def step(k, carry):
+            act(lax.rem(me + far_first(k, n_sub), n_sub))
             return carry
 
-        lax.fori_loop(1, n_sub, step, 0)
+        lax.fori_loop(0, n_sub - 1, step, 0)
 
     def each_passage(act):
-        def step(i, carry):
-            act(lax.rem(myp + i, n_passage))
+        def step(k, carry):
+            act(lax.rem(myp + far_first(k, n_passage), n_passage))
             return carry
 
-        lax.fori_loop(1, n_passage, step, 0)
+        lax.fori_loop(0, n_passage - 1, step, 0)
+
+    def chip_to(t):
+        return lax.rem(chip + far_first(t, chips), chips)
+
+    def chip_from(t):
+        return lax.rem(chip + chips - far_first(t, chips), chips)
 
     v_start()
     departures = [v_sent]
@@ -307,7 +320,7 @@
         return mt[g, 3:4, :] + mt[g, 4:5, :] + mt[g, 5:6, :]
 
     def send_step(t, carry):
-        there = lax.rem(chip + 1 + t, chips)
+        there = chip_to(t)
         parts = [(node_of == mt[2 * there + core, 2:3, :].astype(I32)).astype(F32) for core in range(2)]
         one_hot = jnp.concatenate(parts, axis=1).astype(BF16)
         n2[there] = one_hot
@@ -318,7 +331,7 @@
             values = picked[:, core * 128 : (core + 1) * 128] * weight_row(g)
             for c in range(CHUNKS):
                 out[c, g, 0:MC, :] = values[c * MC : (c + 1) * MC]
-            out[0, g, MC : MC + 8, :] = mt[g]
+            out[0, g, MC : MC + 2, :] = mt[g, 0:2, :]
             pl.when(g != me)(out_copy(0, g, me).start)
         return carry
 
@@ -327,7 +340,8 @@
         each_sub(lambda peer, c=c: out_copy(c, peer, me).start())
     for c in range(CHUNKS):
         departures.append(lambda c=c: each_sub(lambda peer: out_copy(c, peer, me).wait_send()))
-        inc[c, me] = out[c, me]
+        own = MC + 2 if c == 0 else MC
+        inc[c, me, 0:own] = out[c, me, 0:own]
 
     for r in range(2):
         kb = kb_ref[r]
@@ -365,14 +379,18 @@
             j = 2 * there + core
             pl.when(j != me)(functools.partial(act, j))
 
-    def take(c):
-        s[c] = jnp.zeros((CX, CY, MC, CZ), F32)
+    def take(c, first, layers):
+        span = range(2 * layers[0], 2 * layers[0] + 4), range(2 * layers[1], 2 * layers[1] + 4)
+        places = [k for part_of in span for k in part_of]
+        for a in layers:
+            s[c, a : a + 2] = jnp.zeros((2, CY, MC, CZ), F32)
 
         def step(t, carry):
-            there = lax.rem(chip + 2 * chips - 1 - t, chips)
-            each_source(there, lambda j: out_copy(c, j, j).wait_recv())
+            there = chip_from(t)
+            if first:
+                each_source(there, lambda j: out_copy(c, j, j).wait_recv())
             row, column = rows_of(there)
-            if c == 0:
+            if first and c == 0:
                 one_hot = (place == column).astype(F32).astype(BF16)
                 rhot[there] = one_hot
             else:
@@ -380,13 +398,13 @@
             values = jnp.concatenate([inc[c, 2 * there, 0:MC, :], inc[c, 2 * there + 1, 0:MC, :]], axis=1)
             high, low = two(values)
             terms = []
-            for k in range(16):
+            for k in places:
                 mask = jnp.broadcast_to((row == k).astype(F32), (MC, 256)).astype(BF16)
                 terms.append(high * mask)
                 terms.append(low * mask)
             product = nt(jnp.concatenate(terms, axis=0), one_hot)
-            for k in range(16):
-                term = product[2 * k * MC : (2 * k + 1) * MC] + product[(2 * k + 1) * MC : (2 * k + 2) * MC]
+            for n, k in enumerate(places):
+                term = product[2 * n * MC : (2 * n + 1) * MC] + product[(2 * n + 1) * MC : (2 * n + 2) * MC]
                 for q in range(4):
                     s[c, k // 2, (k % 2) * 4 + q] += term[:, q * 128 : (q + 1) * 128]
             return carry
@@ -400,9 +418,10 @@
         passage_copy(s.at[c, pl.ds(0, 2)], xr.at[c], x_send.at[c, 1], x_recv.at[c, 1], left_p) for c in range(CHUNKS)
     ]
     for c in range(CHUNKS):
-        take(c)
+        take(c, True, (0, 6))
         x_right[c].start()
         x_left[c].start()
+        take(c, False, (2, 4))
         departures += [x_right[c].wait_send, x_left[c].wait_send]
 
     s_arrive()
@@ -482,7 +501,7 @@
 
     def give(c):
         def step(t, carry):
-            there = lax.rem(chip + 1 + t, chips)
+            there = chip_to(t)
             row, _ = rows_of(there)
             product = nn(fp[...].reshape(32 * MC, 512), rhot[there])
             total = jnp.zeros((MC, 256), F32)
@@ -506,7 +525,7 @@
 
     def forces(c):
         def step(t, total):
-            there = lax.rem(chip + 2 * chips - 1 - t, chips)
+            there = chip_from(t)
             each_source(there, lambda j: back_copy(c, j, j).wait_recv())
             force = jnp.concatenate([back[c, 2 * there + k] * weight_row(2 * there + k) for k in range(2)], axis=1)
             product = nt(jnp.concatenate(three(force), axis=0), n2[there])
@@ -530,26 +549,29 @@
     product = nt(x_both, z_high) + nt(x_both, z_low)
     product = product[:96] + product[96:]
     third = jnp.where(lane < M, product[0:32, 128:], product[64:96, :128])
-    gram = jnp.concatenate([product[0:64, :128], third, jnp.zeros((32, 128), F32)], axis=0)
+    whole[0:64, :] = product[0:64, :128]
+    whole[64:96, :] = third
+    whole[96:128, :] = jnp.zeros((32, 128), F32)
     for g in range(n_sub):
-        gbuf[g] = gram[g * rows : (g + 1) * rows]
+        gbuf[g, 0:rows, :] = whole[g * rows : (g + 1) * rows, :]
     each_sub(lambda peer: gram_copy(peer, me).start())
     departures.append(lambda: each_sub(lambda peer: gram_copy(peer, me).wait_send()))
-    grecv[me] = gbuf[me]
+    grecv[me, 0:rows] = gbuf[me, 0:rows]
     each_sub(lambda peer: gram_copy(peer, peer).wait_recv())
-    part[0] = lax.fori_loop(1, n_sub, lambda g, total: total + grecv[g], grecv[0])
+    part[0, 0:rows] = lax.fori_loop(1, n_sub, lambda g, total: total + grecv[g, 0:rows], grecv[0, 0:rows])
     each_passage(lambda peer: part_copy(peer, myp).start())
     departures.append(lambda: each_passage(lambda peer: part_copy(peer, myp).wait_send()))
-    precv[myp] = part[0]
+    precv[myp, 0:rows] = part[0, 0:rows]
     each_passage(lambda peer: part_copy(peer, peer).wait_recv())
-    part[1] = lax.fori_loop(1, n_passage, lambda g, total: total + precv[g], precv[0])
+    part[1, 0:rows] = lax.fori_loop(1, n_passage, lambda g, total: total + precv[g, 0:rows], precv[0, 0:rows])
     each_sub(lambda peer: full_copy(peer, me).start())
     departures.append(lambda: each_sub(lambda peer: full_copy(peer, me).wait_send()))
-    gfull[me] = part[1]
+    gfull[me, 0:rows] = part[1, 0:rows]
     each_sub(lambda peer: full_copy(peer, peer).wait_recv())
 
-    whole = jnp.concatenate([gfull[g] for g in range(n_sub)], axis=0)
-    turned = whole.T
+    for g in range(n_sub):
+        whole[g * rows : (g + 1) * rows, :] = gfull[g, 0:rows, :]
+    turned = whole[...].T
     scale = 1.0 / (NSD * n_sub * n_passage)
     row_of = iota((M, 128), 0)
 
@@ -582,6 +604,16 @@
 
     for sent in departures:
         sent()
+
+
+def hand_out(a, b, c, a_out, b_out, c_out, sem):
+    copies = [
+        pltpu.make_async_copy(src, dst, sem.at[k]) for k, (src, dst) in enumerate(((a, a_out), (b, b_out), (c, c_out)))
+    ]
+    for copy in copies:
+        copy.start()
+    for copy in copies:
+        copy.wait()
 
 
 def body(
@@ -600,19 +632,20 @@
 ):
     nc = slot_node.shape[0] // 128
     chips = n_sub // 2
-    rows = 128 // n_sub
+    rows = -(-3 * M // n_sub // 8) * 8
+    shapes = (
+        jax.ShapeDtypeStruct((M, NSD), F32),
+        jax.ShapeDtypeStruct((2 * M, 2 * M), F32),
+        jax.ShapeDtypeStruct((2 * M, 2 * M), F32),
+    )
     vmem = pl.BlockSpec(memory_space=pltpu.VMEM)
     hbm = pl.BlockSpec(memory_space=pltpu.HBM)
     dma = pltpu.SemaphoreType.DMA
     layers = pltpu.VMEM((CHUNKS, 2, CY, MC, CZ), F32)
     cells = pltpu.VMEM((CHUNKS, CX, CY, MC, CZ), F32)
-    return pl.pallas_call(
+    outs = pl.pallas_call(
         functools.partial(kernel, n_passage, n_sub),
-        out_shape=(
-            jax.ShapeDtypeStruct((M, NSD), F32),
-            jax.ShapeDtypeStruct((2 * M, 2 * M), F32),
-            jax.ShapeDtypeStruct((2 * M, 2 * M), F32),
-        ),
+        out_shape=shapes,
         in_specs=[hbm] * 10,
         out_specs=(vmem, vmem, vmem),
         scratch_shapes=[
@@ -654,6 +687,7 @@
             pltpu.VMEM((2, rows, 128), F32),
             pltpu.VMEM((n_passage, rows, 128), F32),
             pltpu.VMEM((n_sub, rows, 128), F32),
+            pltpu.VMEM((128, 128), F32),
             dma((3, 2)),
             dma((3, 2)),
             dma((CHUNKS, n_sub)),
@@ -686,6 +720,13 @@
         slot_weight.reshape(nc, 128),
         live_slots,
     )
+    return pl.pallas_call(
+        hand_out,
+        out_shape=shapes,
+        in_specs=[pl.BlockSpec(memory_space=pl.ANY)] * 3,
+        out_specs=(hbm, hbm, hbm),
+        scratch_shapes=[dma((3,))],
+    )(*outs)
 
 
 def solution(mesh):

time: 78.9 us -> 80.6 us (1.022)
  Pallas kernels: 74.5 us -> 79.2 us
  local copies, waits for them, and re-layouts: 2.77 us -> 0 us
    pallas_call x1 -> x2, Pallas kernels: 74.5 us -> 79.2 us  [the longest x1 75.1 us: body(): pl.pallas_call(functools.partial(kernel, n_passage, n_sub), out_shape=sha...]
    unnamed x7 -> x0, local copies, waits for them, and re-layouts: 2.77 us -> none
where the time goes in v3:
time: 80.6 us; the launch traced here: 80.5 us
  Pallas kernels  79.2 us (98%)
  between operations  1.29 us (2%)
    pallas_call x1, Pallas kernels, body(): pl.pallas_call(functools.partial(kernel, n_passage, n_sub), out_shape=sha...  75.1 us
    pallas_call x1, Pallas kernels, body(): pl.pallas_call(hand_out, out_shape=shapes, in_specs=[pl.BlockSpec(memory_...  4.11 us

profile of v3, /device:TPU:1, one launch (start us, length us, event | category | flops | bytes accessed | tf_op | source)
XLA Modules:
  0.0 80.5 jit_solution(9689376098733216072)
XLA Ops:
  1.3 75.1 %shard_map.121 = (f32[32,256]{1,0:T(8,128)}, f32[64,64]{1,0:T(8,128)}, f32[64,64]{1,0:T(8,128)}) custom-call(f32[32,256]{1,0:T(8,128)} %v_hbm.1, f32[1,256]{1,0:T(1,128)} %bitcast.12, f32[1,256]{1,0:T(1,128)} %bitcast.13, f32[2,512,128]{2,1,0:T(8,128)} %bitcast.7, s32[2,4]{1,0:T(2,128)} %cols_hbm.1, s32[8,128]{1,0:T(8,128)} %bitcast.8, s32[8,128]{1,0:T(8,128)} %bitcast.9, ...), custom_call_target="tpu_custom_call" | custom-call | tf_op jit(solution)/shard_map/pallas_call | solution.py:646
  76.4 4.1 %shard_map.122 = (f32[32,256]{1,0:T(8,128)}, f32[64,64]{1,0:T(8,128)}, f32[64,64]{1,0:T(8,128)}) custom-call(f32[32,256]{1,0:T(8,128)} %get-tuple-element.6.a, f32[64,64]{1,0:T(8,128)} %get-tuple-element.7.b, f32[64,64]{1,0:T(8,128)} %get-tuple-element.8.c), custom_call_target="tpu_custom_call" | custom-call | tf_op jit(solution)/shard_map/pallas_call | solution.py:723

commit v4 on v3

--- a/solution.py
+++ b/solution.py
@@ -101,6 +101,7 @@
     out,
     inc,
     rhot,
+    rowf,
     s,
     xl,
     xr,
@@ -288,6 +289,8 @@
 
     def far_first(k, count):
         half = (k + 1) // 2
+        if isinstance(k, int):
+            return count // 2 + (-half if k % 2 else half)
         return count // 2 + jnp.where(lax.rem(k, 2) == 1, -half, half)
 
     def each_sub(act):
@@ -306,9 +309,6 @@
 
     def chip_to(t):
         return lax.rem(chip + far_first(t, chips), chips)
-
-    def chip_from(t):
-        return lax.rem(chip + chips - far_first(t, chips), chips)
 
     v_start()
     departures = [v_sent]
@@ -336,12 +336,7 @@
         return carry
 
     lax.fori_loop(0, chips, send_step, 0)
-    for c in range(1, CHUNKS):
-        each_sub(lambda peer, c=c: out_copy(c, peer, me).start())
-    for c in range(CHUNKS):
-        departures.append(lambda c=c: each_sub(lambda peer: out_copy(c, peer, me).wait_send()))
-        own = MC + 2 if c == 0 else MC
-        inc[c, me, 0:own] = out[c, me, 0:own]
+    inc[0, me, 0 : MC + 2] = out[0, me, 0 : MC + 2]
 
     for r in range(2):
         kb = kb_ref[r]
@@ -366,6 +361,11 @@
     win_s[3] = image[:, 128:]
     s_start()
     departures.append(s_sent)
+    for c in range(1, CHUNKS):
+        each_sub(lambda peer: out_copy(c - 1, peer, me).wait_send())
+        each_sub(lambda peer: out_copy(c, peer, me).start())
+        inc[c, me, 0:MC] = out[c, me, 0:MC]
+    departures.append(lambda: each_sub(lambda peer: out_copy(CHUNKS - 1, peer, me).wait_send()))
 
     place = iota((512, 256), 0)
 
@@ -379,37 +379,30 @@
             j = 2 * there + core
             pl.when(j != me)(functools.partial(act, j))
 
-    def take(c, first, layers):
-        span = range(2 * layers[0], 2 * layers[0] + 4), range(2 * layers[1], 2 * layers[1] + 4)
-        places = [k for part_of in span for k in part_of]
-        for a in layers:
-            s[c, a : a + 2] = jnp.zeros((2, CY, MC, CZ), F32)
-
-        def step(t, carry):
-            there = chip_from(t)
-            if first:
-                each_source(there, lambda j: out_copy(c, j, j).wait_recv())
-            row, column = rows_of(there)
-            if first and c == 0:
-                one_hot = (place == column).astype(F32).astype(BF16)
-                rhot[there] = one_hot
-            else:
-                one_hot = rhot[there]
-            values = jnp.concatenate([inc[c, 2 * there, 0:MC, :], inc[c, 2 * there + 1, 0:MC, :]], axis=1)
-            high, low = two(values)
-            terms = []
-            for k in places:
-                mask = jnp.broadcast_to((row == k).astype(F32), (MC, 256)).astype(BF16)
-                terms.append(high * mask)
-                terms.append(low * mask)
-            product = nt(jnp.concatenate(terms, axis=0), one_hot)
-            for n, k in enumerate(places):
-                term = product[2 * n * MC : (2 * n + 1) * MC] + product[(2 * n + 1) * MC : (2 * n + 2) * MC]
-                for q in range(4):
-                    s[c, k // 2, (k % 2) * 4 + q] += term[:, q * 128 : (q + 1) * 128]
-            return carry
-
-        lax.fori_loop(0, chips, step, 0)
+    def take(c):
+        each_sub(lambda peer: out_copy(c, peer, peer).wait_recv())
+        if c == 0:
+
+            def mark(there, carry):
+                row, column = rows_of(there)
+                rhot[there] = (place == column).astype(F32).astype(BF16)
+                rowf[there] = jnp.broadcast_to(row, (8, 256))
+                return carry
+
+            lax.fori_loop(0, chips, mark, 0)
+        one_hot = jnp.concatenate([rhot[k] for k in range(chips)], axis=1)
+        row = jnp.concatenate([rowf[k, 0:1, :] for k in range(chips)], axis=1)
+        high, low = two(jnp.concatenate([inc[c, k, 0:MC, :] for k in range(n_sub)], axis=1))
+        highs, lows = [], []
+        for k in range(16):
+            mask = jnp.broadcast_to((row == k).astype(F32), (MC, n_sub * CAP)).astype(BF16)
+            highs.append(high * mask)
+            lows.append(low * mask)
+        terms = jnp.concatenate([jnp.concatenate(highs, axis=0), jnp.concatenate(lows, axis=0)], axis=1)
+        product = nt(terms, jnp.concatenate([one_hot, one_hot], axis=1))
+        for k in range(16):
+            for q in range(4):
+                s[c, k // 2, (k % 2) * 4 + q] = product[k * MC : (k + 1) * MC, q * 128 : (q + 1) * 128]
 
     x_right = [
         passage_copy(s.at[c, pl.ds(6, 2)], xl.at[c], x_send.at[c, 0], x_recv.at[c, 0], right_p) for c in range(CHUNKS)
@@ -418,22 +411,22 @@
         passage_copy(s.at[c, pl.ds(0, 2)], xr.at[c], x_send.at[c, 1], x_recv.at[c, 1], left_p) for c in range(CHUNKS)
     ]
     for c in range(CHUNKS):
-        take(c, True, (0, 6))
+        take(c)
         x_right[c].start()
         x_left[c].start()
-        take(c, False, (2, 4))
         departures += [x_right[c].wait_send, x_left[c].wait_send]
 
     s_arrive()
     image_image = apply(win_s, image)
 
     lane = iota((M, 128), 1)
-    chunk_lane = iota((MC, 128), 1)
-    inner_low = (chunk_lane > 0).astype(F32) * 0.5
-    inner_high = (chunk_lane < 127).astype(F32) * 0.5
-
-    def along(x):
-        return x + pltpu.roll(x, 1, 1) * inner_low + pltpu.roll(x, 127, 1) * inner_high
+    apart = jnp.abs(iota((128, 128), 0) - iota((128, 128), 1))
+    at_end = (iota((128, 128), 0) == 0) | (iota((128, 128), 0) == 127)
+    once = jnp.where(apart == 0, 1.0, jnp.where(apart == 1, 0.5, 0.0))
+    middle_weight = jnp.where(at_end, 1.25, 1.5)
+    twice = jnp.where(apart == 0, middle_weight, jnp.where(apart == 1, 1.0, jnp.where(apart == 2, 0.25, 0.0)))
+    once = jnp.concatenate([once, once], axis=0).astype(BF16)
+    twice = jnp.concatenate([twice, twice], axis=0).astype(BF16)
 
     def filters(c, layers):
         def layer(a, b):
@@ -443,16 +436,21 @@
                 return xr[c, a - CX, b]
             return s[c, a, b]
 
-        def step(b, carry):
-            for a in layers:
+        ps, qs = [], []
+        for a in layers:
+            for b in range(CY):
                 near = layer(a - 1, b) + layer(a + 1, b)
                 mine = layer(a, b)
                 far = layer(a - 2, b) + layer(a + 2, b)
-                pp[c, a, b] = BETA * along(mine + 0.5 * near)
-                qq[c, a, b] = GAMMA * along(along(1.5 * mine + near + 0.25 * far))
-            return carry
-
-        lax.fori_loop(0, CY, step, 0)
+                ps.append(jnp.concatenate(two(mine + 0.5 * near), axis=1))
+                qs.append(jnp.concatenate(two(1.5 * mine + near + 0.25 * far), axis=1))
+        p = BETA * nn(jnp.concatenate(ps, axis=0), once)
+        q = GAMMA * nn(jnp.concatenate(qs, axis=0), twice)
+        for n, a in enumerate(layers):
+            for b in range(CY):
+                at = (n * CY + b) * MC
+                pp[c, a, b] = p[at : at + MC]
+                qq[c, a, b] = q[at : at + MC]
 
     y_right = [sub_copy(ysr.at[c], yl.at[c], y_send.at[c, 0], y_recv.at[c, 0], me + 1) for c in range(CHUNKS)]
     y_left = [sub_copy(ysl.at[c], yr.at[c], y_send.at[c, 1], y_recv.at[c, 1], me - 1) for c in range(CHUNKS)]
@@ -462,14 +460,11 @@
         x_left[c].wait_recv()
         filters(c, (0, 1, 6, 7))
 
-        def edge_step(a, carry):
+        for a in range(CX):
             ysr[c, 0, a] = 0.5 * pp[c, a, 7] + 0.25 * qq[c, a, 6] + qq[c, a, 7]
             ysr[c, 1, a] = 0.25 * qq[c, a, 7]
             ysl[c, 0, a] = 0.5 * pp[c, a, 0] + 0.25 * qq[c, a, 1] + qq[c, a, 0]
             ysl[c, 1, a] = 0.25 * qq[c, a, 0]
-            return carry
-
-        lax.fori_loop(0, CX, edge_step, 0)
         pl.when(has_right)(y_right[c].start)
         pl.when(has_left)(y_left[c].start)
         departures.append(lambda c=c: pl.when(has_right)(y_right[c].wait_send))
@@ -493,27 +488,27 @@
                 if b >= CY - 2:
                     total = total + yr[c, CY - 1 - b, a]
                 high, low = two(total)
-                fp[0, 2 * a + b // 4, :, (b % 4) * 128 : (b % 4 + 1) * 128] = high
-                fp[1, 2 * a + b // 4, :, (b % 4) * 128 : (b % 4 + 1) * 128] = low
+                fp[2 * a + b // 4, :, (b % 4) * 128 : (b % 4 + 1) * 128] = high
+                fp[2 * a + b // 4, :, 512 + (b % 4) * 128 : 512 + (b % 4 + 1) * 128] = low
             return carry
 
         lax.fori_loop(0, CX, step, 0)
 
     def give(c):
-        def step(t, carry):
-            there = chip_to(t)
-            row, _ = rows_of(there)
-            product = nn(fp[...].reshape(32 * MC, 512), rhot[there])
-            total = jnp.zeros((MC, 256), F32)
-            for k in range(16):
-                both = product[k * MC : (k + 1) * MC] + product[(16 + k) * MC : (17 + k) * MC]
-                total = total + jnp.where(row == k, both, 0.0)
-            for core in range(2):
-                ret[c, 2 * there + core] = total[:, core * 128 : (core + 1) * 128]
-            each_source(there, lambda j: back_copy(c, j, me).start())
-            return carry
-
-        lax.fori_loop(0, chips, step, 0)
+        fields = fp[...].reshape(16 * MC, 1024)
+        for times in (range(chips // 2), range(chips // 2, chips)):
+            one_hot = jnp.concatenate([rhot[chip_to(t)] for t in times], axis=1)
+            row = jnp.concatenate([rowf[chip_to(t), 0:1, :] for t in times], axis=1)
+            product = nn(fields, jnp.concatenate([one_hot, one_hot], axis=0))
+            total = jnp.where(row == 0, product[0:MC], 0.0)
+            for k in range(1, 16):
+                total = jnp.where(row == k, product[k * MC : (k + 1) * MC], total)
+            for n, t in enumerate(times):
+                for core in range(2):
+                    at = (2 * n + core) * 128
+                    ret[c, 2 * chip_to(t) + core] = total[:, at : at + 128]
+            for t in times:
+                each_source(chip_to(t), lambda j: back_copy(c, j, me).start())
         back[c, me] = ret[c, me]
 
     for c in range(CHUNKS):
@@ -524,14 +519,11 @@
         departures.append(lambda c=c: each_sub(lambda peer: back_copy(c, peer, me).wait_send()))
 
     def forces(c):
-        def step(t, total):
-            there = chip_from(t)
-            each_source(there, lambda j: back_copy(c, j, j).wait_recv())
-            force = jnp.concatenate([back[c, 2 * there + k] * weight_row(2 * there + k) for k in range(2)], axis=1)
-            product = nt(jnp.concatenate(three(force), axis=0), n2[there])
-            return total + product[0:MC] + product[MC : 2 * MC] + product[2 * MC :]
-
-        return lax.fori_loop(0, chips, step, mass_ref[...] * v[c * MC : (c + 1) * MC])
+        each_sub(lambda peer: back_copy(c, peer, peer).wait_recv())
+        force = jnp.concatenate([back[c, k] * weight_row(k) for k in range(n_sub)], axis=1)
+        product = nt(jnp.concatenate(three(force), axis=0), jnp.concatenate([n2[k] for k in range(chips)], axis=1))
+        product = product[0:MC] + product[MC : 2 * MC] + product[2 * MC :]
+        return mass_ref[...] * v[c * MC : (c + 1) * MC] + product
 
     massed = jnp.concatenate([forces(c) for c in range(CHUNKS)], axis=0)
     win_w[2] = massed[:, :128]
@@ -606,16 +598,6 @@
         sent()
 
 
-def hand_out(a, b, c, a_out, b_out, c_out, sem):
-    copies = [
-        pltpu.make_async_copy(src, dst, sem.at[k]) for k, (src, dst) in enumerate(((a, a_out), (b, b_out), (c, c_out)))
-    ]
-    for copy in copies:
-        copy.start()
-    for copy in copies:
-        copy.wait()
-
-
 def body(
     n_passage,
     n_sub,
@@ -643,7 +625,7 @@
     dma = pltpu.SemaphoreType.DMA
     layers = pltpu.VMEM((CHUNKS, 2, CY, MC, CZ), F32)
     cells = pltpu.VMEM((CHUNKS, CX, CY, MC, CZ), F32)
-    outs = pl.pallas_call(
+    return pl.pallas_call(
         functools.partial(kernel, n_passage, n_sub),
         out_shape=shapes,
         in_specs=[hbm] * 10,
@@ -670,6 +652,7 @@
             pltpu.VMEM((CHUNKS, n_sub, MC + 8, CAP), F32),
             pltpu.VMEM((CHUNKS, n_sub, MC + 8, CAP), F32),
             pltpu.VMEM((chips, 512, 256), BF16),
+            pltpu.VMEM((chips, 8, 256), I32),
             cells,
             layers,
             layers,
@@ -679,7 +662,7 @@
             layers,
             layers,
             layers,
-            pltpu.VMEM((2, 16, MC, 512), BF16),
+            pltpu.VMEM((16, MC, 1024), BF16),
             pltpu.VMEM((CHUNKS, n_sub, MC, CAP), F32),
             pltpu.VMEM((CHUNKS, n_sub, MC, CAP), F32),
             pltpu.VMEM((n_sub, rows, 128), F32),
@@ -720,13 +703,6 @@
         slot_weight.reshape(nc, 128),
         live_slots,
     )
-    return pl.pallas_call(
-        hand_out,
-        out_shape=shapes,
-        in_specs=[pl.BlockSpec(memory_space=pl.ANY)] * 3,
-        out_specs=(hbm, hbm, hbm),
-        scratch_shapes=[dma((3,))],
-    )(*outs)
 
 
 def solution(mesh):

time: 80.6 us -> 73.1 us (0.907)
  Pallas kernels: 79.2 us -> 68.8 us
  local copies, waits for them, and re-layouts: 0 us -> 2.77 us
    pallas_call x1, Pallas kernels: 75.1 us -> 68.8 us  [body(): pl.pallas_call(functools.partial(kernel, n_passage, n_sub), out_shape=sha...]
    pallas_call x1 -> x0, Pallas kernels: 4.11 us -> none  [body(): pl.pallas_call(hand_out, out_shape=shapes, in_specs=[pl.BlockSpec(memory_...]
    unnamed x0 -> x7, local copies, waits for them, and re-layouts: none -> 2.77 us
where the time goes in v4:
time: 73.1 us; the launch traced here: 72.9 us
  Pallas kernels  68.8 us (94%)
  local copies, waits for them, and re-layouts  2.77 us (4%)
  between operations  1.3 us (2%)
    pallas_call x1, Pallas kernels, body(): pl.pallas_call(functools.partial(kernel, n_passage, n_sub), out_shape=sha...  68.8 us
    unnamed x7, local copies, waits for them, and re-layouts  2.77 us

profile of v4, /device:TPU:1, one launch (start us, length us, event | category | flops | bytes accessed | tf_op | source)
XLA Modules:
  0.0 72.9 jit_solution(72246635310471398)
XLA Ops:
  1.3 68.8 %shard_map.121 = (f32[32,256]{1,0:T(8,128)}, f32[64,64]{1,0:T(8,128)}, f32[64,64]{1,0:T(8,128)}) custom-call(f32[32,256]{1,0:T(8,128)} %v_hbm.1, f32[1,256]{1,0:T(1,128)} %bitcast.12, f32[1,256]{1,0:T(1,128)} %bitcast.13, f32[2,512,128]{2,1,0:T(8,128)} %bitcast.7, s32[2,4]{1,0:T(2,128)} %cols_hbm.1, s32[8,128]{1,0:T(8,128)} %bitcast.8, s32[8,128]{1,0:T(8,128)} %bitcast.9, ...), custom_call_target="tpu_custom_call" | custom-call | tf_op jit(solution)/shard_map/pallas_call | solution.py:628
  70.1 0.0 copy-start.1
  70.1 1.4 %copy.17 = f32[32,256]{1,0:T(8,128)} copy(f32[32,256]{1,0:T(8,128)} %get-tuple-element.6) | data formatting | bytes 65536
  71.5 0.0 copy-done.1
  71.5 0.0 copy-start
  71.5 0.6 copy.18
  72.1 0.2 copy-done
  72.3 0.6 copy.19
Async XLA Ops:
  70.1 1.4 %copy-start.1 = (f32[64,64]{1,0:T(8,128)S(1)}, f32[64,64]{1,0:T(8,128)}, u32[]{:S(2)}) copy-start(f32[64,64]{1,0:T(8,128)} %get-tuple-element.7) | copy-start | bytes 49156
  71.5 0.8 %copy-start = (f32[64,64]{1,0:T(8,128)S(1)}, f32[64,64]{1,0:T(8,128)}, u32[]{:S(2)}) copy-start(f32[64,64]{1,0:T(8,128)} %get-tuple-element.8) | copy-start | bytes 49156

commit v5 on v4

--- a/solution.py
+++ b/solution.py
@@ -191,16 +191,16 @@
 
     barrier = pltpu.get_barrier_semaphore()
 
-    def greet_sub(i, carry):
+    def greet_sub(i):
         pl.semaphore_signal(barrier, inc=1, device_id={"sub": lax.rem(me + i, n_sub)}, device_id_type=MESH)
-        return carry
-
-    def greet_passage(i, carry):
+
+    def greet_passage(i):
         pl.semaphore_signal(barrier, inc=1, device_id={"passage": lax.rem(myp + i, n_passage)}, device_id_type=MESH)
-        return carry
-
-    lax.fori_loop(1, n_sub, greet_sub, 0)
-    lax.fori_loop(1, n_passage, greet_passage, 0)
+
+    for i in range(1, n_sub):
+        greet_sub(i)
+    for i in range(1, n_passage):
+        greet_passage(i)
 
     for load in loads[:5]:
         load.wait()
@@ -289,23 +289,15 @@
 
     def far_first(k, count):
         half = (k + 1) // 2
-        if isinstance(k, int):
-            return count // 2 + (-half if k % 2 else half)
-        return count // 2 + jnp.where(lax.rem(k, 2) == 1, -half, half)
+        return count // 2 + (-half if k % 2 else half)
 
     def each_sub(act):
-        def step(k, carry):
+        for k in range(n_sub - 1):
             act(lax.rem(me + far_first(k, n_sub), n_sub))
-            return carry
-
-        lax.fori_loop(0, n_sub - 1, step, 0)
 
     def each_passage(act):
-        def step(k, carry):
+        for k in range(n_passage - 1):
             act(lax.rem(myp + far_first(k, n_passage), n_passage))
-            return carry
-
-        lax.fori_loop(0, n_passage - 1, step, 0)
 
     def chip_to(t):
         return lax.rem(chip + far_first(t, chips), chips)
@@ -319,7 +311,7 @@
     def weight_row(g):
         return mt[g, 3:4, :] + mt[g, 4:5, :] + mt[g, 5:6, :]
 
-    def send_step(t, carry):
+    def send_step(t):
         there = chip_to(t)
         parts = [(node_of == mt[2 * there + core, 2:3, :].astype(I32)).astype(F32) for core in range(2)]
         one_hot = jnp.concatenate(parts, axis=1).astype(BF16)
@@ -333,9 +325,9 @@
                 out[c, g, 0:MC, :] = values[c * MC : (c + 1) * MC]
             out[0, g, MC : MC + 2, :] = mt[g, 0:2, :]
             pl.when(g != me)(out_copy(0, g, me).start)
-        return carry
-
-    lax.fori_loop(0, chips, send_step, 0)
+
+    for t in range(chips):
+        send_step(t)
     inc[0, me, 0 : MC + 2] = out[0, me, 0 : MC + 2]
 
     for r in range(2):
@@ -383,13 +375,10 @@
         each_sub(lambda peer: out_copy(c, peer, peer).wait_recv())
         if c == 0:
 
-            def mark(there, carry):
+            for there in range(chips):
                 row, column = rows_of(there)
                 rhot[there] = (place == column).astype(F32).astype(BF16)
                 rowf[there] = jnp.broadcast_to(row, (8, 256))
-                return carry
-
-            lax.fori_loop(0, chips, mark, 0)
         one_hot = jnp.concatenate([rhot[k] for k in range(chips)], axis=1)
         row = jnp.concatenate([rowf[k, 0:1, :] for k in range(chips)], axis=1)
         high, low = two(jnp.concatenate([inc[c, k, 0:MC, :] for k in range(n_sub)], axis=1))
@@ -550,12 +539,12 @@
     departures.append(lambda: each_sub(lambda peer: gram_copy(peer, me).wait_send()))
     grecv[me, 0:rows] = gbuf[me, 0:rows]
     each_sub(lambda peer: gram_copy(peer, peer).wait_recv())
-    part[0, 0:rows] = lax.fori_loop(1, n_sub, lambda g, total: total + grecv[g, 0:rows], grecv[0, 0:rows])
+    part[0, 0:rows] = sum(grecv[g, 0:rows] for g in range(n_sub))
     each_passage(lambda peer: part_copy(peer, myp).start())
     departures.append(lambda: each_passage(lambda peer: part_copy(peer, myp).wait_send()))
     precv[myp, 0:rows] = part[0, 0:rows]
     each_passage(lambda peer: part_copy(peer, peer).wait_recv())
-    part[1, 0:rows] = lax.fori_loop(1, n_passage, lambda g, total: total + precv[g, 0:rows], precv[0, 0:rows])
+    part[1, 0:rows] = sum(precv[g, 0:rows] for g in range(n_passage))
     each_sub(lambda peer: full_copy(peer, me).start())
     departures.append(lambda: each_sub(lambda peer: full_copy(peer, me).wait_send()))
     gfull[me, 0:rows] = part[1, 0:rows]

time: 73.1 us -> 71.2 us (0.974)
  Pallas kernels: 68.8 us -> 66.9 us
    pallas_call x1, Pallas kernels: 68.8 us -> 66.9 us  [body(): pl.pallas_call(functools.partial(kernel, n_passage, n_sub), out_shape=sha...]
where the time goes in v5:
time: 71.2 us; the launch traced here: 71 us
  Pallas kernels  66.9 us (94%)
  local copies, waits for them, and re-layouts  2.77 us (4%)
  between operations  1.3 us (2%)
    pallas_call x1, Pallas kernels, body(): pl.pallas_call(functools.partial(kernel, n_passage, n_sub), out_shape=sha...  66.9 us
    unnamed x7, local copies, waits for them, and re-layouts  2.77 us

profile of v5, /device:TPU:1, one launch (start us, length us, event | category | flops | bytes accessed | tf_op | source)
XLA Modules:
  0.0 71.0 jit_solution(4185140172379396939)
XLA Ops:
  1.3 66.9 %shard_map.121 = (f32[32,256]{1,0:T(8,128)}, f32[64,64]{1,0:T(8,128)}, f32[64,64]{1,0:T(8,128)}) custom-call(f32[32,256]{1,0:T(8,128)} %v_hbm.1, f32[1,256]{1,0:T(1,128)} %bitcast.12, f32[1,256]{1,0:T(1,128)} %bitcast.13, f32[2,512,128]{2,1,0:T(8,128)} %bitcast.7, s32[2,4]{1,0:T(2,128)} %cols_hbm.1, s32[8,128]{1,0:T(8,128)} %bitcast.8, s32[8,128]{1,0:T(8,128)} %bitcast.9, ...), custom_call_target="tpu_custom_call" | custom-call | tf_op jit(solution)/shard_map/pallas_call | solution.py:617
  68.2 0.0 copy-start.1
  68.2 1.4 %copy.17 = f32[32,256]{1,0:T(8,128)} copy(f32[32,256]{1,0:T(8,128)} %get-tuple-element.6) | data formatting | bytes 65536
  69.6 0.0 copy-done.1
  69.6 0.0 copy-start
  69.6 0.6 copy.18
  70.2 0.2 copy-done
  70.4 0.6 copy.19
Async XLA Ops:
  68.2 1.4 %copy-start.1 = (f32[64,64]{1,0:T(8,128)S(1)}, f32[64,64]{1,0:T(8,128)}, u32[]{:S(2)}) copy-start(f32[64,64]{1,0:T(8,128)} %get-tuple-element.7) | copy-start | bytes 49156
  69.6 0.8 %copy-start = (f32[64,64]{1,0:T(8,128)S(1)}, f32[64,64]{1,0:T(8,128)}, u32[]{:S(2)}) copy-start(f32[64,64]{1,0:T(8,128)} %get-tuple-element.8) | copy-start | bytes 49156

commit v6 on v4

--- a/solution.py
+++ b/solution.py
@@ -298,14 +298,16 @@
             act(lax.rem(me + far_first(k, n_sub), n_sub))
             return carry
 
-        lax.fori_loop(0, n_sub - 1, step, 0)
+        for k in range(n_sub - 1):
+            step(k, 0)
 
     def each_passage(act):
         def step(k, carry):
             act(lax.rem(myp + far_first(k, n_passage), n_passage))
             return carry
 
-        lax.fori_loop(0, n_passage - 1, step, 0)
+        for k in range(n_passage - 1):
+            step(k, 0)
 
     def chip_to(t):
         return lax.rem(chip + far_first(t, chips), chips)
@@ -550,12 +552,12 @@
     departures.append(lambda: each_sub(lambda peer: gram_copy(peer, me).wait_send()))
     grecv[me, 0:rows] = gbuf[me, 0:rows]
     each_sub(lambda peer: gram_copy(peer, peer).wait_recv())
-    part[0, 0:rows] = lax.fori_loop(1, n_sub, lambda g, total: total + grecv[g, 0:rows], grecv[0, 0:rows])
+    part[0, 0:rows] = sum(grecv[g, 0:rows] for g in range(n_sub))
     each_passage(lambda peer: part_copy(peer, myp).start())
     departures.append(lambda: each_passage(lambda peer: part_copy(peer, myp).wait_send()))
     precv[myp, 0:rows] = part[0, 0:rows]
     each_passage(lambda peer: part_copy(peer, peer).wait_recv())
-    part[1, 0:rows] = lax.fori_loop(1, n_passage, lambda g, total: total + precv[g, 0:rows], precv[0, 0:rows])
+    part[1, 0:rows] = sum(precv[g, 0:rows] for g in range(n_passage))
     each_sub(lambda peer: full_copy(peer, me).start())
     departures.append(lambda: each_sub(lambda peer: full_copy(peer, me).wait_send()))
     gfull[me, 0:rows] = part[1, 0:rows]

time: 73.1 us -> 70.3 us (0.962)
  Pallas kernels: 68.8 us -> 66 us
    pallas_call x1, Pallas kernels: 68.8 us -> 66 us  [body(): pl.pallas_call(functools.partial(kernel, n_passage, n_sub), out_shape=sha...]
where the time goes in v6:
time: 70.3 us; the launch traced here: 70 us
  Pallas kernels  66 us (94%)
  local copies, waits for them, and re-layouts  2.77 us (4%)
  between operations  1.3 us (2%)
    pallas_call x1, Pallas kernels, body(): pl.pallas_call(functools.partial(kernel, n_passage, n_sub), out_shape=sha...  66 us
    unnamed x7, local copies, waits for them, and re-layouts  2.77 us

profile of v6, /device:TPU:1, one launch (start us, length us, event | category | flops | bytes accessed | tf_op | source)
XLA Modules:
  0.0 70.0 jit_solution(11709601608110391582)
XLA Ops:
  1.3 66.0 %shard_map.121 = (f32[32,256]{1,0:T(8,128)}, f32[64,64]{1,0:T(8,128)}, f32[64,64]{1,0:T(8,128)}) custom-call(f32[32,256]{1,0:T(8,128)} %v_hbm.1, f32[1,256]{1,0:T(1,128)} %bitcast.12, f32[1,256]{1,0:T(1,128)} %bitcast.13, f32[2,512,128]{2,1,0:T(8,128)} %bitcast.7, s32[2,4]{1,0:T(2,128)} %cols_hbm.1, s32[8,128]{1,0:T(8,128)} %bitcast.8, s32[8,128]{1,0:T(8,128)} %bitcast.9, ...), custom_call_target="tpu_custom_call" | custom-call | tf_op jit(solution)/shard_map/pallas_call | solution.py:630
  67.2 0.0 copy-start.1
  67.3 1.4 %copy.17 = f32[32,256]{1,0:T(8,128)} copy(f32[32,256]{1,0:T(8,128)} %get-tuple-element.6) | data formatting | bytes 65536
  68.6 0.0 copy-done.1
  68.6 0.0 copy-start
  68.6 0.6 copy.18
  69.3 0.2 copy-done
  69.4 0.6 copy.19
Async XLA Ops:
  67.2 1.4 %copy-start.1 = (f32[64,64]{1,0:T(8,128)S(1)}, f32[64,64]{1,0:T(8,128)}, u32[]{:S(2)}) copy-start(f32[64,64]{1,0:T(8,128)} %get-tuple-element.7) | copy-start | bytes 49156
  68.6 0.8 %copy-start = (f32[64,64]{1,0:T(8,128)S(1)}, f32[64,64]{1,0:T(8,128)}, u32[]{:S(2)}) copy-start(f32[64,64]{1,0:T(8,128)} %get-tuple-element.8) | copy-start | bytes 49156

commit v7 on v6

--- a/solution.py
+++ b/solution.py
@@ -302,12 +302,11 @@
             step(k, 0)
 
     def each_passage(act):
-        def step(k, carry):
-            act(lax.rem(myp + far_first(k, n_passage), n_passage))
-            return carry
-
-        for k in range(n_passage - 1):
-            step(k, 0)
+        def hops(i):
+            return min(i // 8, 4 - i // 8) + min(i % 8, 8 - i % 8)
+
+        for i in sorted(range(1, n_passage), key=hops, reverse=True):
+            act(lax.rem(myp + i, n_passage))
 
     def chip_to(t):
         return lax.rem(chip + far_first(t, chips), chips)
@@ -549,17 +548,23 @@
     for g in range(n_sub):
         gbuf[g, 0:rows, :] = whole[g * rows : (g + 1) * rows, :]
     each_sub(lambda peer: gram_copy(peer, me).start())
-    departures.append(lambda: each_sub(lambda peer: gram_copy(peer, me).wait_send()))
+    for sent in departures:
+        sent()
+    departures = [lambda: each_sub(lambda peer: gram_copy(peer, me).wait_send())]
     grecv[me, 0:rows] = gbuf[me, 0:rows]
     each_sub(lambda peer: gram_copy(peer, peer).wait_recv())
     part[0, 0:rows] = sum(grecv[g, 0:rows] for g in range(n_sub))
     each_passage(lambda peer: part_copy(peer, myp).start())
-    departures.append(lambda: each_passage(lambda peer: part_copy(peer, myp).wait_send()))
+    for sent in departures:
+        sent()
+    departures = [lambda: each_passage(lambda peer: part_copy(peer, myp).wait_send())]
     precv[myp, 0:rows] = part[0, 0:rows]
     each_passage(lambda peer: part_copy(peer, peer).wait_recv())
     part[1, 0:rows] = sum(precv[g, 0:rows] for g in range(n_passage))
     each_sub(lambda peer: full_copy(peer, me).start())
-    departures.append(lambda: each_sub(lambda peer: full_copy(peer, me).wait_send()))
+    for sent in departures:
+        sent()
+    departures = [lambda: each_sub(lambda peer: full_copy(peer, me).wait_send())]
     gfull[me, 0:rows] = part[1, 0:rows]
     each_sub(lambda peer: full_copy(peer, peer).wait_recv())
 

time: 70.3 us -> 70.1 us (level)
  no operation moved by 1% of the time
where the time goes in v7:
time: 70.1 us; the launch traced here: 69.9 us
  Pallas kernels  65.8 us (94%)
  local copies, waits for them, and re-layouts  2.77 us (4%)
  between operations  1.3 us (2%)
    pallas_call x1, Pallas kernels, body(): pl.pallas_call(functools.partial(kernel, n_passage, n_sub), out_shape=sha...  65.8 us
    unnamed x7, local copies, waits for them, and re-layouts  2.77 us

profile of v7, /device:TPU:1, one launch (start us, length us, event | category | flops | bytes accessed | tf_op | source)
XLA Modules:
  0.0 69.9 jit_solution(4093765376564459001)
XLA Ops:
  1.3 65.8 %shard_map.121 = (f32[32,256]{1,0:T(8,128)}, f32[64,64]{1,0:T(8,128)}, f32[64,64]{1,0:T(8,128)}) custom-call(f32[32,256]{1,0:T(8,128)} %v_hbm.1, f32[1,256]{1,0:T(1,128)} %bitcast.12, f32[1,256]{1,0:T(1,128)} %bitcast.13, f32[2,512,128]{2,1,0:T(8,128)} %bitcast.7, s32[2,4]{1,0:T(2,128)} %cols_hbm.1, s32[8,128]{1,0:T(8,128)} %bitcast.8, s32[8,128]{1,0:T(8,128)} %bitcast.9, ...), custom_call_target="tpu_custom_call" | custom-call | tf_op jit(solution)/shard_map/pallas_call | solution.py:635
  67.1 0.0 copy-start.1
  67.1 1.4 %copy.17 = f32[32,256]{1,0:T(8,128)} copy(f32[32,256]{1,0:T(8,128)} %get-tuple-element.6) | data formatting | bytes 65536
  68.5 0.0 copy-done.1
  68.5 0.0 copy-start
  68.5 0.6 copy.18
  69.1 0.2 copy-done
  69.3 0.6 copy.19
Async XLA Ops:
  67.1 1.4 %copy-start.1 = (f32[64,64]{1,0:T(8,128)S(1)}, f32[64,64]{1,0:T(8,128)}, u32[]{:S(2)}) copy-start(f32[64,64]{1,0:T(8,128)} %get-tuple-element.7) | copy-start | bytes 49156
  68.5 0.8 %copy-start = (f32[64,64]{1,0:T(8,128)S(1)}, f32[64,64]{1,0:T(8,128)}, u32[]{:S(2)}) copy-start(f32[64,64]{1,0:T(8,128)} %get-tuple-element.8) | copy-start | bytes 49156
